TPU v7x, 512 devices: a whole 4x8x8 slice. The times are simulated.
512 devices in a mesh: prow: 32 (over x_lo, z, core), pcol: 16 (over y, x_hi).
Axes of the slice: x: 4 (x_hi: 2, x_lo: 2; x = x_hi * 2 + x_lo), y: 8, z: 8, core: 2. Of those that a mesh axis runs over, the one named last changes fastest.
Arguments:
- reduced_vectors: float32 [98304, 2048], P('prow', 'pcol'), may hold values from -6 to 6
- panel_one: float32 [98304, 256], P(('prow', 'pcol')), may hold values from -0.01953125 to 0.01953125
- factor_one: float32 [256, 256], P('pcol'), as said below
- panel_two: float32 [98304, 256], P(('prow', 'pcol')), may hold values from -0.01953125 to 0.01953125
- factor_two: float32 [256, 256], P('pcol'), as said below
Outputs:
- eigenvectors: float32 [98304, 2048], P('prow', 'pcol')
Inputs may be any that keep to these rules, and one draw needn't show every extreme that they name: factor_one is upper triangular with its diagonal between 1 and 2. factor_two is upper triangular with its diagonal between 1 and 2.
All inputs are finite; a program needn't handle non-finite values.
Results may differ from a plain program's by a relative error of at most 0.00007.
Values sent between devices are 32-bit elements; how exact they have to be, the bound alone decides.
No kernel may reach another device: no remote copies, remote signals or barrier semaphores. Data moves between devices by JAX's collectives and lax.ppermute only.
A program may use at most 64 MiB of HBM per device.

v0:
```python
import jax
import jax.numpy as jnp
from jax import lax
from jax.sharding import PartitionSpec as P


def matmul_hi(left, right):
    return jnp.dot(left, right, precision=lax.Precision.HIGHEST, preferred_element_type=jnp.float32)


def inner_prod(left, right):
    return lax.dot_general(
        left,
        right,
        (((0,), (0,)), ((), ())),
        precision=lax.Precision.HIGHEST,
        preferred_element_type=jnp.float32,
    )


def combine(partial_value, applier):
    return applier(lax.psum(partial_value, "prow"))


def shards(reduced_vectors, panel_one, factor_one, panel_two, factor_two):
    current = reduced_vectors
    sections = ((panel_two, factor_two), (panel_one, factor_one))
    for position in range(2):
        section_vec, section_tri = sections[position]
        left_vec, tri_full = (
            lax.all_gather(section_vec, "pcol", axis=0, tiled=True),
            lax.all_gather(section_tri, "pcol", axis=0, tiled=True),
        )
        partial_value = inner_prod(left_vec, current)
        coeffs = combine(partial_value, lambda moment: matmul_hi(tri_full, moment))
        current = current - matmul_hi(left_vec, coeffs)
    return current


def solution(mesh):
    in_specs = (
        P("prow", "pcol"),
        P(("prow", "pcol"), None),
        P("pcol", None),
        P(("prow", "pcol"), None),
        P("pcol", None),
    )
    out_specs = P("prow", "pcol")
    return jax.shard_map(shards, mesh=mesh, in_specs=in_specs, out_specs=out_specs, check_vma=False)
```

profile of v0, /device:TPU:1, one launch (start us, length us, event | category | flops | bytes accessed | tf_op | source)
XLA Modules:
  0.0 647.7 jit_solution(12528842017722275619)
XLA Ops:
  6.5 0.0 all-gather.3.cloned.1.call-start
  6.5 0.7 all-gather.3.cloned.1.call-update
  7.3 0.0 copy-start
  7.3 0.0 all-reduce.3.cloned.1.call-start
  7.3 103.9 %all-gather.3.cloned.1.call-done = f32[3072,256]{1,0:T(8,128)} async-done(((f32[192,256]{1,0:T(8,128)}), f32[3072,256]{1,0:T(8,128)}) %all-gather.3.cloned.1.call-update) | async-done | bytes 3145744 | tf_op jit(solution)/shard_map/all_gather | solution.py:31
  111.2 8.0 %fusion.2 = f32[256,128]{1,0:T(8,128)} fusion(f32[3072,256]{1,0:T(8,128)} %all-gather.3.cloned.1.call-done, f32[3072,128]{1,0:T(8,128)} %param.5), kind=kOutput, calls=%fused_computation.5 | convolution fusion | flops 1207959552 | bytes 4849664 | tf_op jit(solution)/shard_map/dot_general | solution.py:12
  119.2 0.0 all-reduce.3.cloned.1.call-update
  119.3 0.0 all-gather.5.cloned.1.call-start
  119.3 0.7 all-gather.5.cloned.1.call-update
  120.0 0.0 copy-start.1
  120.0 0.0 all-reduce.5.cloned.1.call-start
  120.1 0.0 copy-done
  120.1 0.5 copy.6
  120.5 0.2 copy-done.1
  120.7 31.5 %all_gather.13 = f32[256,256]{1,0:T(8,128)S(1)} all-gather(f32[16,256]{1,0:T(8,128)S(1)} %copy-done.1), channel_id=1, replica_groups=mesh['prow'=32,'pcol'=16] {'pcol'}, dimensions={0}, use_global_device_ids=true | all-gather | bytes 278528 | tf_op jit(solution)/shard_map/all_gather | solution.py:32
  152.3 173.3 %all-reduce.3.cloned.1.call-done = f32[256,128]{1,0:T(8,128)} async-done(((f32[256,128]{1,0:T(8,128)}), f32[256,128]{1,0:T(8,128)}) %all-reduce.3.cloned.1.call-update) | async-done | bytes 131088 | tf_op jit(solution)/shard_map/psum | solution.py:22
  325.5 1.3 fusion.3
  326.8 5.1 fusion
  332.0 0.0 copy-start.2
  332.0 90.8 %all-gather.5.cloned.1.call-done = f32[3072,256]{1,0:T(8,128)} async-done(((f32[192,256]{1,0:T(8,128)}), f32[3072,256]{1,0:T(8,128)}) %all-gather.5.cloned.1.call-update) | async-done | bytes 3145744 | tf_op jit(solution)/shard_map/all_gather | solution.py:31
  422.8 4.2 convolution_bitcast_fusion.2
  427.0 0.0 all-reduce.5.cloned.1.call-update
  427.0 0.0 copy-done.2
  427.0 31.7 %all_gather.15 = f32[256,256]{1,0:T(8,128)S(1)} all-gather(f32[16,256]{1,0:T(8,128)S(1)} %copy-done.2), channel_id=1, replica_groups=mesh['prow'=32,'pcol'=16] {'pcol'}, dimensions={0}, use_global_device_ids=true | all-gather | bytes 278528 | tf_op jit(solution)/shard_map/all_gather | solution.py:32
  458.7 174.4 %all-reduce.5.cloned.1.call-done = f32[256,128]{0,1:T(8,128)} async-done(((f32[256,128]{0,1:T(8,128)}), f32[256,128]{0,1:T(8,128)}) %all-reduce.5.cloned.1.call-update) | async-done | bytes 131088 | tf_op jit(solution)/shard_map/psum | solution.py:22
  633.1 1.3 fusion.4
  634.4 5.1 fusion.1
  639.6 1.6 copy.7
Async XLA Ops:
  6.5 104.7 %all-gather.3.cloned.1.call-start = ((), (), s32[]{:S(2)}) async-start(), calls=%async_computation | async-start | bytes 3342336 | tf_op jit(solution)/shard_map/all_gather | solution.py:31
  7.3 112.8 %copy-start = (f32[3072,128]{1,0:T(8,128)S(1)}, f32[3072,128]{1,0:T(8,128)}, u32[]{:S(2)}) copy-start(f32[3072,128]{1,0:T(8,128)} %param.5) | copy-start | bytes 4718596
  7.3 318.3 %all-reduce.3.cloned.1.call-start = ((), (), s32[]{:S(2)}) async-start(), calls=%async_computation.1 | async-start | bytes 262144 | tf_op jit(solution)/shard_map/psum | solution.py:22
  119.3 303.6 %all-gather.5.cloned.1.call-start = ((), (), s32[]{:S(2)}) async-start(), calls=%async_computation.2 | async-start | bytes 3342336 | tf_op jit(solution)/shard_map/all_gather | solution.py:31
  120.0 0.7 copy-start.1
  120.0 513.1 %all-reduce.5.cloned.1.call-start = ((), (), s32[]{:S(2)}) async-start(), calls=%async_computation.3 | async-start | bytes 262144 | tf_op jit(solution)/shard_map/psum | solution.py:22
  332.0 95.0 %copy-start.2 = (f32[16,256]{1,0:T(8,128)S(1)}, f32[16,256]{1,0:T(8,128)}, u32[]{:S(2)}) copy-start(f32[16,256]{1,0:T(8,128)} %param.7) | copy-start | bytes 49156
Sparse Core Ops, SparseCore 0:
  10.5 100.6 all-gather.2
  119.4 206.1 all-reduce.2
  329.2 93.5 all-gather.4
  427.1 205.9 all-reduce.4
where the time goes:
time: 648 us
  waiting for transfers between devices  544 us (84%)
  blocking collectives  63.3 us (10%)
  matrix products  25.1 us (4%)
  between operations  13.2 us (2%)
    psum x2, waiting for transfers between devices, combine(): return applier(lax.psum(partial_value, 'prow'))  348 us
    all_gather x2, waiting for transfers between devices, shards(): lax.all_gather(section_vec, 'pcol', axis=0, tiled=True)  195 us
    all_gather x2, blocking collectives, shards(): lax.all_gather(section_tri, 'pcol', axis=0, tiled=True)  63.3 us
  transfers between devices with their start and end apart: 4, of which 4 were waited for; matrix products, arithmetic and copies ran while one was open for 1% of the time, Pallas kernels for 0%

commit v1 on v0

v1 whole, which is shorter than its diff:
```python
import jax
import jax.numpy as jnp
from jax import lax
from jax.sharding import Mesh
from jax.sharding import PartitionSpec as P

AXES = ("xl", "z", "core", "y", "xh")
SIZES = (2, 8, 2, 8, 2)
NY = 8


def dot(left, right, dims):
    return lax.dot_general(
        left,
        right,
        (dims, ((), ())),
        precision=lax.Precision.HIGH,
        preferred_element_type=jnp.float32,
    )


def swap(value, axis):
    return lax.ppermute(value, axis, [(0, 1), (1, 0)])


def step_up(value):
    return lax.ppermute(value, "y", [(i, (i + 1) % NY) for i in range(NY)])


def step_down(value):
    return lax.ppermute(value, "y", [(i, (i - 1) % NY) for i in range(NY)])


def pair_up(own):
    other = swap(own, "xh")
    first = lax.axis_index("xh") == 0
    return jnp.stack([jnp.where(first, own, other), jnp.where(first, other, own)])


def ring(own):
    blocks = [None] * NY
    blocks[0] = own
    up = down = own
    for step in range(1, 4):
        up, down = step_up(up), step_down(down)
        blocks[NY - step], blocks[step] = up, down
    low, high = step_up(up[0]), step_down(down[1])
    blocks[4] = jnp.stack([low, high])
    return blocks


def all_sum(partial_value):
    rows = partial_value.shape[0] // 16
    parts = lax.all_to_all(
        partial_value.reshape(16, rows, 128), ("z", "core"), 0, 0
    ).sum(0)
    parts = parts + swap(parts, "xl")
    spread = jnp.broadcast_to(parts[None], (16, rows, 128))
    return lax.all_to_all(spread, ("z", "core"), 0, 0).reshape(16 * rows, 128)


def shards(vectors, panel_one, factor_one, panel_two, factor_two):
    here = lax.axis_index("y")
    rows = panel_one.shape[0]
    two = ring(pair_up(jnp.concatenate([panel_two, factor_two])))
    one = ring(pair_up(jnp.concatenate([panel_one, factor_one])))

    by_owner = vectors.reshape(NY, 2, rows, 128)
    rolled = lax.dynamic_slice_in_dim(
        jnp.concatenate([by_owner, by_owner]), here, NY, 0
    )
    both = ((0, 1), (0, 1))
    inner_two = inner_one = cross = 0.0
    for k in range(NY):
        part_two, part_one = two[k][:, :rows], one[k][:, :rows]
        inner_two = inner_two + dot(part_two, rolled[k], both)
        inner_one = inner_one + dot(part_one, rolled[k], both)
        cross = cross + dot(part_one, part_two, both)
    sums = all_sum(
        jnp.concatenate([inner_two, inner_one, cross[:, :128], cross[:, 128:]])
    )
    inner_two, inner_one = sums[:256], sums[256:512]
    cross = jnp.concatenate([sums[512:768], sums[768:]], axis=1)

    def whole(blocks):
        tri = jnp.concatenate([b[:, rows:].reshape(-1, 256) for b in blocks])
        tri = jnp.concatenate([tri, tri])
        return lax.dynamic_slice_in_dim(tri, (NY - here) % NY * 32, 256, 0)

    plain = ((1,), (0,))
    coeff_two = dot(whole(two), inner_two, plain)
    coeff_one = dot(whole(one), inner_one - dot(cross, coeff_two, plain), plain)
    out = [
        rolled[k]
        - dot(two[k][:, :rows], coeff_two, ((2,), (0,)))
        - dot(one[k][:, :rows], coeff_one, ((2,), (0,)))
        for k in range(NY)
    ]
    out = jnp.stack(out + out)
    out = lax.dynamic_slice_in_dim(out, (NY - here) % NY, NY, 0)
    return out.reshape(vectors.shape)


def solution(mesh):
    fine = Mesh(mesh.devices.reshape(SIZES), AXES)
    prow, pcol = ("xl", "z", "core"), ("y", "xh")
    in_specs = (
        P(prow, pcol),
        P(prow + pcol, None),
        P(pcol, None),
        P(prow + pcol, None),
        P(pcol, None),
    )
    return jax.shard_map(
        shards,
        mesh=fine,
        in_specs=in_specs,
        out_specs=P(prow, pcol),
        check_vma=False,
    )
```

time: 648 us -> 178 us (0.27)
  waiting for transfers between devices: 544 us -> 30.7 us
  starting transfers between devices: 0.12 us -> 84.2 us
  blocking collectives: 63.3 us -> 0 us
  local copies, waits for them, and re-layouts: 2.27 us -> 35.2 us
  between operations: 13.2 us -> 1.39 us
    psum x2 -> x0, waiting for transfers between devices: 348 us -> none  [combine(): return applier(lax.psum(partial_value, 'prow'))]
    all_gather x2 -> x0, waiting for transfers between devices: 195 us -> none  [shards(): lax.all_gather(section_vec, 'pcol', axis=0, tiled=True)]
    all_gather x2 -> x0, blocking collectives: 63.3 us -> none  [shards(): lax.all_gather(section_tri, 'pcol', axis=0, tiled=True)]
    ppermute x0 -> x19, starting transfers between devices: none -> 61.7 us  [the longest x8 36.6 us: step_down(): return lax.ppermute(value, 'y', [(i, (i - 1) % NY) for i in range(NY)])]
    unnamed x7 -> x115, local copies, waits for them, and re-layouts: 0.66 us -> 25.7 us
    all_to_all x0 -> x2, starting transfers between devices: none -> 22.5 us  [the longest x1 18.4 us: all_sum(): lax.all_to_all(partial_value.reshape(16, rows, 128), ('z', 'core'), 0, 0)]
    ppermute x0 -> x19, waiting for transfers between devices: none -> 18.4 us  [the longest x8 9.19 us: step_up(): return lax.ppermute(value, 'y', [(i, (i + 1) % NY) for i in range(NY)])]
    all_to_all x0 -> x2, waiting for transfers between devices: none -> 12.3 us  [the longest x1 6.48 us: all_sum(): return lax.all_to_all(spread, ('z', 'core'), 0, 0).reshape(16 * rows, 128)]
  transfers between devices with their start and end apart: 4 -> 21, of which waited for: 4 -> 7; matrix products, arithmetic and copies ran while one was open for 1% -> 23% of each run, Pallas kernels for 0% -> 0%
where the time goes in v1:
time: 178 us; the launch traced here: 176 us
  starting transfers between devices  84.2 us (47%)
  local copies, waits for them, and re-layouts  35.2 us (20%)
  waiting for transfers between devices  30.7 us (17%)
  matrix products  19.3 us (11%)
  other arithmetic  5.08 us (3%)
    ppermute x8, starting transfers between devices, step_down(): return lax.ppermute(value, 'y', [(i, (i - 1) % NY) for i in range(NY)])  36.6 us
    unnamed x115, local copies, waits for them, and re-layouts  25.7 us
    dot_general x43, matrix products, dot(): lax.dot_general(left, right, (dims, ((), ())), precision=lax.Precision.HI...  19.3 us
    all_to_all x1, starting transfers between devices, all_sum(): lax.all_to_all(partial_value.reshape(16, rows, 128), ('z', 'core'), 0, 0)  18.4 us
    ppermute x8, starting transfers between devices, step_up(): return lax.ppermute(value, 'y', [(i, (i + 1) % NY) for i in range(NY)])  15.5 us
    ppermute x3, starting transfers between devices, swap(): return lax.ppermute(value, axis, [(0, 1), (1, 0)])  9.59 us
    ppermute x8, waiting for transfers between devices, step_up(): return lax.ppermute(value, 'y', [(i, (i + 1) % NY) for i in range(NY)])  9.19 us
    ppermute x3, waiting for transfers between devices, swap(): return lax.ppermute(value, axis, [(0, 1), (1, 0)])  8.03 us
  transfers between devices with their start and end apart: 21, of which 7 were waited for; matrix products, arithmetic and copies ran while one was open for 23% of the time, Pallas kernels for 0%

profile of v1, /device:TPU:1, one launch (start us, length us, event | category | flops | bytes accessed | tf_op | source)
XLA Modules:
  0.0 175.9 jit_solution(16256037204378506951)
XLA Ops:
  1.7 5.5 %collective-permute-start.9 = (f32[208,256]{1,0:T(8,128)S(1)}, f32[208,256]{1,0:T(8,128)S(1)}, u32[]{:S(2)}, u32[]{:S(2)}) collective-permute-start(f32[208,256]{1,0:T(8,128)S(1)} %constant_dynamic-update-slice_fusion.18), channel_id=1, source_target_pairs={{0,1},{1,0},{2,3},{3,2},{4,5},{5,4},{6,7},{7,6},{8,9},{9,8},{10,11... | collective-permute-start | bytes 638984 | tf_op jit(solution)/shard_map/ppermute | solution.py:23
  8.8 1.9 %collective-permute-start = (f32[208,256]{1,0:T(8,128)S(1)}, f32[208,256]{1,0:T(8,128)S(1)}, u32[]{:S(2)}, u32[]{:S(2)}) collective-permute-start(f32[208,256]{1,0:T(8,128)S(1)} %constant_dynamic-update-slice_fusion), channel_id=1, source_target_pairs={{0,1},{1,0},{2,3},{3,2},{4,5},{5,4},{6,7},{7,6},{8,9},{9,8},{10,11... | collective-permute-start | bytes 638984 | tf_op jit(solution)/shard_map/ppermute | solution.py:23
  10.8 1.7 fusion
  12.5 6.8 %collective-permute-done = f32[208,256]{1,0:T(8,128)S(1)} collective-permute-done((f32[208,256]{1,0:T(8,128)S(1)}, f32[208,256]{1,0:T(8,128)S(1)}, u32[]{:S(2)}, u32[]{:S(2)}) %collective-permute-start) | collective-permute-done | bytes 213024 | tf_op jit(solution)/shard_map/ppermute | solution.py:23
  19.4 3.8 %collective-permute-start.1 = (f32[2,208,256]{2,1,0:T(8,128)S(1)}, f32[2,208,256]{2,1,0:T(8,128)S(1)}, u32[]{:S(2)}, u32[]{:S(2)}) collective-permute-start(f32[2,208,256]{2,1,0:T(8,128)S(1)} %pad_maximum_fusion), channel_id=1, source_target_pairs={{0,14},{2,0},{4,2},{6,4},{8,6},{10,8},{12,10},{14,12},{1,15},{3,1}... | collective-permute-start | bytes 1277960 | tf_op jit(solution)/shard_map/ppermute | solution.py:31
  23.2 1.9 %collective-permute-start.4 = (f32[2,208,256]{2,1,0:T(8,128)S(1)}, f32[2,208,256]{2,1,0:T(8,128)S(1)}, u32[]{:S(2)}, u32[]{:S(2)}) collective-permute-start(f32[2,208,256]{2,1,0:T(8,128)S(1)} %pad_maximum_fusion), channel_id=1, source_target_pairs={{0,2},{2,4},{4,6},{6,8},{8,10},{10,12},{12,14},{14,0},{1,3},{3,5},... | collective-permute-start | bytes 1277960 | tf_op jit(solution)/shard_map/ppermute | solution.py:27
  25.1 4.6 %collective-permute-start.10 = (f32[2,208,256]{2,1,0:T(8,128)S(1)}, f32[2,208,256]{2,1,0:T(8,128)S(1)}, u32[]{:S(2)}, u32[]{:S(2)}) collective-permute-start(f32[2,208,256]{2,1,0:T(8,128)S(1)} %pad_maximum_fusion.1), channel_id=1, source_target_pairs={{0,14},{2,0},{4,2},{6,4},{8,6},{10,8},{12,10},{14,12},{1,15},{3,1}... | collective-permute-start | bytes 1277960 | tf_op jit(solution)/shard_map/ppermute | solution.py:31
  29.7 1.9 %collective-permute-start.13 = (f32[2,208,256]{2,1,0:T(8,128)S(1)}, f32[2,208,256]{2,1,0:T(8,128)S(1)}, u32[]{:S(2)}, u32[]{:S(2)}) collective-permute-start(f32[2,208,256]{2,1,0:T(8,128)S(1)} %pad_maximum_fusion.1), channel_id=1, source_target_pairs={{0,2},{2,4},{4,6},{6,8},{8,10},{10,12},{12,14},{14,0},{1,3},{3,5},... | collective-permute-start | bytes 1277960 | tf_op jit(solution)/shard_map/ppermute | solution.py:27
  33.8 4.6 %collective-permute-start.2 = (f32[2,208,256]{2,1,0:T(8,128)S(1)}, f32[2,208,256]{2,1,0:T(8,128)S(1)}, u32[]{:S(2)}, u32[]{:S(2)}) collective-permute-start(f32[2,208,256]{2,1,0:T(8,128)S(1)} %collective-permute-done.1), channel_id=1, source_target_pairs={{0,14},{2,0},{4,2},{6,4},{8,6},{10,8},{12,10},{14,12},{1,15},{3,1}... | collective-permute-start | bytes 1277960 | tf_op jit(solution)/shard_map/ppermute | solution.py:31
  39.5 5.3 %collective-permute-start.11 = (f32[2,208,256]{2,1,0:T(8,128)S(1)}, f32[2,208,256]{2,1,0:T(8,128)S(1)}, u32[]{:S(2)}, u32[]{:S(2)}) collective-permute-start(f32[2,208,256]{2,1,0:T(8,128)S(1)} %collective-permute-done.10), channel_id=1, source_target_pairs={{0,14},{2,0},{4,2},{6,4},{8,6},{10,8},{12,10},{14,12},{1,15},{3,1}... | collective-permute-start | bytes 1277960 | tf_op jit(solution)/shard_map/ppermute | solution.py:31
  44.9 1.9 %collective-permute-start.14 = (f32[2,208,256]{2,1,0:T(8,128)S(1)}, f32[2,208,256]{2,1,0:T(8,128)S(1)}, u32[]{:S(2)}, u32[]{:S(2)}) collective-permute-start(f32[2,208,256]{2,1,0:T(8,128)S(1)} %collective-permute-done.13), channel_id=1, source_target_pairs={{0,2},{2,4},{4,6},{6,8},{8,10},{10,12},{12,14},{14,0},{1,3},{3,5},... | collective-permute-start | bytes 1277960 | tf_op jit(solution)/shard_map/ppermute | solution.py:27
  47.4 1.9 %collective-permute-start.5 = (f32[2,208,256]{2,1,0:T(8,128)S(1)}, f32[2,208,256]{2,1,0:T(8,128)S(1)}, u32[]{:S(2)}, u32[]{:S(2)}) collective-permute-start(f32[2,208,256]{2,1,0:T(8,128)S(1)} %collective-permute-done.4), channel_id=1, source_target_pairs={{0,2},{2,4},{4,6},{6,8},{8,10},{10,12},{12,14},{14,0},{1,3},{3,5},... | collective-permute-start | bytes 1277960 | tf_op jit(solution)/shard_map/ppermute | solution.py:27
  53.2 4.6 %collective-permute-start.3 = (f32[2,208,256]{2,1,0:T(8,128)S(1)}, f32[2,208,256]{2,1,0:T(8,128)S(1)}, u32[]{:S(2)}, u32[]{:S(2)}) collective-permute-start(f32[2,208,256]{2,1,0:T(8,128)S(1)} %collective-permute-done.2), channel_id=1, source_target_pairs={{0,14},{2,0},{4,2},{6,4},{8,6},{10,8},{12,10},{14,12},{1,15},{3,1}... | collective-permute-start | bytes 1277960 | tf_op jit(solution)/shard_map/ppermute | solution.py:31
  57.8 5.2 %collective-permute-done.5 = f32[2,208,256]{2,1,0:T(8,128)S(1)} collective-permute-done((f32[2,208,256]{2,1,0:T(8,128)S(1)}, f32[2,208,256]{2,1,0:T(8,128)S(1)}, u32[]{:S(2)}, u32[]{:S(2)}) %collective-permute-start.5) | collective-permute-done | bytes 426016 | tf_op jit(solution)/shard_map/ppermute | solution.py:27
  63.6 1.9 %collective-permute-start.6 = (f32[2,208,256]{2,1,0:T(8,128)S(1)}, f32[2,208,256]{2,1,0:T(8,128)S(1)}, u32[]{:S(2)}, u32[]{:S(2)}) collective-permute-start(f32[2,208,256]{2,1,0:T(8,128)S(1)} %collective-permute-done.5), channel_id=1, source_target_pairs={{0,2},{2,4},{4,6},{6,8},{8,10},{10,12},{12,14},{14,0},{1,3},{3,5},... | collective-permute-start | bytes 1277960 | tf_op jit(solution)/shard_map/ppermute | solution.py:27
  65.6 4.6 %collective-permute-start.12 = (f32[2,208,256]{2,1,0:T(8,128)S(1)}, f32[2,208,256]{2,1,0:T(8,128)S(1)}, u32[]{:S(2)}, u32[]{:S(2)}) collective-permute-start(f32[2,208,256]{2,1,0:T(8,128)S(1)} %collective-permute-done.11), channel_id=1, source_target_pairs={{0,14},{2,0},{4,2},{6,4},{8,6},{10,8},{12,10},{14,12},{1,15},{3,1}... | collective-permute-start | bytes 1277960 | tf_op jit(solution)/shard_map/ppermute | solution.py:31
  70.2 1.9 %collective-permute-start.15 = (f32[2,208,256]{2,1,0:T(8,128)S(1)}, f32[2,208,256]{2,1,0:T(8,128)S(1)}, u32[]{:S(2)}, u32[]{:S(2)}) collective-permute-start(f32[2,208,256]{2,1,0:T(8,128)S(1)} %collective-permute-done.14), channel_id=1, source_target_pairs={{0,2},{2,4},{4,6},{6,8},{8,10},{10,12},{12,14},{14,0},{1,3},{3,5},... | collective-permute-start | bytes 1277960 | tf_op jit(solution)/shard_map/ppermute | solution.py:27
  76.0 4.6 %collective-permute-start.8 = (f32[208,256]{1,0:T(8,128)S(1)}, f32[208,256]{1,0:T(8,128)S(1)}, u32[]{:S(2)}, u32[]{:S(2)}) collective-permute-start(f32[208,256]{1,0:T(8,128)S(1)} %slice_bitcast_fusion.2), channel_id=1, source_target_pairs={{0,14},{2,0},{4,2},{6,4},{8,6},{10,8},{12,10},{14,12},{1,15},{3,1}... | collective-permute-start | bytes 638984 | tf_op jit(solution)/shard_map/ppermute | solution.py:31
  80.6 1.9 %collective-permute-start.7 = (f32[208,256]{1,0:T(8,128)S(1)}, f32[208,256]{1,0:T(8,128)S(1)}, u32[]{:S(2)}, u32[]{:S(2)}) collective-permute-start(f32[208,256]{1,0:T(8,128)S(1)} %slice_bitcast_fusion.3), channel_id=1, source_target_pairs={{0,2},{2,4},{4,6},{6,8},{8,10},{10,12},{12,14},{14,0},{1,3},{3,5},... | collective-permute-start | bytes 638984 | tf_op jit(solution)/shard_map/ppermute | solution.py:27
  82.6 4.6 %collective-permute-start.17 = (f32[208,256]{1,0:T(8,128)S(1)}, f32[208,256]{1,0:T(8,128)S(1)}, u32[]{:S(2)}, u32[]{:S(2)}) collective-permute-start(f32[208,256]{1,0:T(8,128)S(1)} %slice_bitcast_fusion), channel_id=1, source_target_pairs={{0,14},{2,0},{4,2},{6,4},{8,6},{10,8},{12,10},{14,12},{1,15},{3,1}... | collective-permute-start | bytes 638984 | tf_op jit(solution)/shard_map/ppermute | solution.py:31
  87.2 2.1 %collective-permute-start.16 = (f32[208,256]{1,0:T(8,128)S(1)}, f32[208,256]{1,0:T(8,128)S(1)}, u32[]{:S(2)}, u32[]{:S(2)}) collective-permute-start(f32[208,256]{1,0:T(8,128)S(1)} %slice_bitcast_fusion.1), channel_id=1, source_target_pairs={{0,2},{2,4},{4,6},{6,8},{8,10},{10,12},{12,14},{14,0},{1,3},{3,5},... | collective-permute-start | bytes 638984 | tf_op jit(solution)/shard_map/ppermute | solution.py:27
  92.2 4.0 %collective-permute-done.16 = f32[208,256]{1,0:T(8,128)S(1)} collective-permute-done((f32[208,256]{1,0:T(8,128)S(1)}, f32[208,256]{1,0:T(8,128)S(1)}, u32[]{:S(2)}, u32[]{:S(2)}) %collective-permute-start.16) | collective-permute-done | bytes 213024 | tf_op jit(solution)/shard_map/ppermute | solution.py:27
  100.4 18.4 %all-to-all-start = ((f32[16,64,128]{2,1,0:T(8,128)}), f32[16,64,128]{2,1,0:T(8,128)}, u32[]{:S(2)}, u32[]{:S(2)}) async-start(f32[16,64,128]{2,1,0:T(8,128)} %bitcast.258), calls=%async_computation | async-start | bytes 1048576 | tf_op jit(solution)/shard_map/all_to_all | solution.py:54
  118.8 1.4 constant_dynamic-update-slice_fusion.26
  120.1 1.4 constant_dynamic-update-slice_fusion.25
  121.5 1.4 constant_dynamic-update-slice_fusion.24
  122.9 1.4 constant_dynamic-update-slice_fusion.23
  124.2 1.4 constant_dynamic-update-slice_fusion.22
  125.6 1.4 constant_dynamic-update-slice_fusion.21
  127.0 1.4 constant_dynamic-update-slice_fusion.20
  128.9 1.4 constant_dynamic-update-slice_fusion.12
  130.3 5.9 %all-to-all-done = f32[16,64,128]{2,1,0:T(8,128)} async-done(((f32[16,64,128]{2,1,0:T(8,128)}), f32[16,64,128]{2,1,0:T(8,128)}, u32[]{:S(2)}, u32[]{:S(2)}) %all-to-all-start) | async-done | bytes 524320 | tf_op jit(solution)/shard_map/all_to_all | solution.py:54
  136.2 1.7 reduce_sum.9
  137.9 2.2 %collective-permute-start.18 = (f32[64,128]{1,0:T(8,128)}, f32[64,128]{1,0:T(8,128)S(1)}, u32[]{:S(2)}, u32[]{:S(2)}) collective-permute-start(f32[64,128]{1,0:T(8,128)} %reduce_sum.9), channel_id=1, source_target_pairs={{0,256},{256,0},{1,257},{257,1},{2,258},{258,2},{3,259},{259,3},{4... | collective-permute-start | bytes 98312 | tf_op jit(solution)/shard_map/ppermute | solution.py:23
  140.1 1.4 constant_dynamic-update-slice_fusion.11
  141.5 1.3 collective-permute-done.18
  144.3 4.1 %all-to-all-start.1 = ((f32[16,64,128]{2,1,0:T(8,128)}), f32[16,64,128]{2,1,0:T(8,128)}, u32[]{:S(2)}, u32[]{:S(2)}) async-start(f32[16,64,128]{2,1,0:T(8,128)} %broadcast_in_dim.2), calls=%async_computation.1 | async-start | bytes 1048576 | tf_op jit(solution)/shard_map/all_to_all | solution.py:59
  148.5 1.4 constant_dynamic-update-slice_fusion.10
  150.5 1.4 constant_dynamic-update-slice_fusion.8
  151.9 1.4 constant_dynamic-update-slice_fusion.7
  153.2 1.4 constant_dynamic-update-slice_fusion.6
  155.2 1.4 constant_dynamic-update-slice_fusion.4
  156.6 1.4 constant_dynamic-update-slice_fusion.3
  158.0 1.4 constant_dynamic-update-slice_fusion.2
  159.3 6.5 %all-to-all-done.1 = f32[16,64,128]{2,1,0:T(8,128)} async-done(((f32[16,64,128]{2,1,0:T(8,128)}), f32[16,64,128]{2,1,0:T(8,128)}, u32[]{:S(2)}, u32[]{:S(2)}) %all-to-all-start.1) | async-done | bytes 524320 | tf_op jit(solution)/shard_map/all_to_all | solution.py:59
  165.8 1.2 fusion.117
  167.1 1.3 fusion.87
  174.7 1.3 constant_dynamic-slice_fusion
  (189 shorter events, 31.7 us)
Async XLA Ops:
  1.7 10.8 %collective-permute-start.9 = (f32[208,256]{1,0:T(8,128)S(1)}, f32[208,256]{1,0:T(8,128)S(1)}, u32[]{:S(2)}, u32[]{:S(2)}) collective-permute-start(f32[208,256]{1,0:T(8,128)S(1)} %constant_dynamic-update-slice_fusion.18), channel_id=1, source_target_pairs={{0,1},{1,0},{2,3},{3,2},{4,5},{5,4},{6,7},{7,6},{8,9},{9,8},{10,11... | collective-permute-start | bytes 638984 | tf_op jit(solution)/shard_map/ppermute | solution.py:23
  8.8 10.5 %collective-permute-start = (f32[208,256]{1,0:T(8,128)S(1)}, f32[208,256]{1,0:T(8,128)S(1)}, u32[]{:S(2)}, u32[]{:S(2)}) collective-permute-start(f32[208,256]{1,0:T(8,128)S(1)} %constant_dynamic-update-slice_fusion), channel_id=1, source_target_pairs={{0,1},{1,0},{2,3},{3,2},{4,5},{5,4},{6,7},{7,6},{8,9},{9,8},{10,11... | collective-permute-start | bytes 638984 | tf_op jit(solution)/shard_map/ppermute | solution.py:23
  19.4 14.4 %collective-permute-start.1 = (f32[2,208,256]{2,1,0:T(8,128)S(1)}, f32[2,208,256]{2,1,0:T(8,128)S(1)}, u32[]{:S(2)}, u32[]{:S(2)}) collective-permute-start(f32[2,208,256]{2,1,0:T(8,128)S(1)} %pad_maximum_fusion), channel_id=1, source_target_pairs={{0,14},{2,0},{4,2},{6,4},{8,6},{10,8},{12,10},{14,12},{1,15},{3,1}... | collective-permute-start | bytes 1277960 | tf_op jit(solution)/shard_map/ppermute | solution.py:31
  23.2 24.2 %collective-permute-start.4 = (f32[2,208,256]{2,1,0:T(8,128)S(1)}, f32[2,208,256]{2,1,0:T(8,128)S(1)}, u32[]{:S(2)}, u32[]{:S(2)}) collective-permute-start(f32[2,208,256]{2,1,0:T(8,128)S(1)} %pad_maximum_fusion), channel_id=1, source_target_pairs={{0,2},{2,4},{4,6},{6,8},{8,10},{10,12},{12,14},{14,0},{1,3},{3,5},... | collective-permute-start | bytes 1277960 | tf_op jit(solution)/shard_map/ppermute | solution.py:27
  25.1 14.4 %collective-permute-start.10 = (f32[2,208,256]{2,1,0:T(8,128)S(1)}, f32[2,208,256]{2,1,0:T(8,128)S(1)}, u32[]{:S(2)}, u32[]{:S(2)}) collective-permute-start(f32[2,208,256]{2,1,0:T(8,128)S(1)} %pad_maximum_fusion.1), channel_id=1, source_target_pairs={{0,14},{2,0},{4,2},{6,4},{8,6},{10,8},{12,10},{14,12},{1,15},{3,1}... | collective-permute-start | bytes 1277960 | tf_op jit(solution)/shard_map/ppermute | solution.py:31
  29.7 15.2 %collective-permute-start.13 = (f32[2,208,256]{2,1,0:T(8,128)S(1)}, f32[2,208,256]{2,1,0:T(8,128)S(1)}, u32[]{:S(2)}, u32[]{:S(2)}) collective-permute-start(f32[2,208,256]{2,1,0:T(8,128)S(1)} %pad_maximum_fusion.1), channel_id=1, source_target_pairs={{0,2},{2,4},{4,6},{6,8},{8,10},{10,12},{12,14},{14,0},{1,3},{3,5},... | collective-permute-start | bytes 1277960 | tf_op jit(solution)/shard_map/ppermute | solution.py:27
  33.8 38.9 %copy-start.8 = (f32[2,208,256]{2,1,0:T(8,128)}, f32[2,208,256]{2,1,0:T(8,128)S(1)}, u32[]{:S(2)}) copy-start(f32[2,208,256]{2,1,0:T(8,128)S(1)} %collective-permute-done.1) | copy-start | bytes 1277956
  33.8 18.3 %copy-start.27 = (f32[2,16,256]{2,1,0:T(8,128)}, f32[2,16,256]{2,1,0:T(8,128)S(1)}, u32[]{:S(2)}) copy-start(f32[2,16,256]{2,1,0:T(8,128)S(1)} %slice.253) | copy-start | bytes 98308
  33.8 19.3 %collective-permute-start.2 = (f32[2,208,256]{2,1,0:T(8,128)S(1)}, f32[2,208,256]{2,1,0:T(8,128)S(1)}, u32[]{:S(2)}, u32[]{:S(2)}) collective-permute-start(f32[2,208,256]{2,1,0:T(8,128)S(1)} %collective-permute-done.1), channel_id=1, source_target_pairs={{0,14},{2,0},{4,2},{6,4},{8,6},{10,8},{12,10},{14,12},{1,15},{3,1}... | collective-permute-start | bytes 1277960 | tf_op jit(solution)/shard_map/ppermute | solution.py:31
  39.5 33.1 %copy-start.10 = (f32[2,208,256]{2,1,0:T(8,128)}, f32[2,208,256]{2,1,0:T(8,128)S(1)}, u32[]{:S(2)}) copy-start(f32[2,208,256]{2,1,0:T(8,128)S(1)} %collective-permute-done.10) | copy-start | bytes 1277956
  39.5 12.6 %copy-start.29 = (f32[2,16,256]{2,1,0:T(8,128)}, f32[2,16,256]{2,1,0:T(8,128)S(1)}, u32[]{:S(2)}) copy-start(f32[2,16,256]{2,1,0:T(8,128)S(1)} %slice.291) | copy-start | bytes 98308
  39.5 26.0 %collective-permute-start.11 = (f32[2,208,256]{2,1,0:T(8,128)S(1)}, f32[2,208,256]{2,1,0:T(8,128)S(1)}, u32[]{:S(2)}, u32[]{:S(2)}) collective-permute-start(f32[2,208,256]{2,1,0:T(8,128)S(1)} %collective-permute-done.10), channel_id=1, source_target_pairs={{0,14},{2,0},{4,2},{6,4},{8,6},{10,8},{12,10},{14,12},{1,15},{3,1}... | collective-permute-start | bytes 1277960 | tf_op jit(solution)/shard_map/ppermute | solution.py:31
  44.9 25.3 %copy-start.6 = (f32[2,208,256]{2,1,0:T(8,128)}, f32[2,208,256]{2,1,0:T(8,128)S(1)}, u32[]{:S(2)}) copy-start(f32[2,208,256]{2,1,0:T(8,128)S(1)} %collective-permute-done.13) | copy-start | bytes 1277956
  44.9 25.3 %collective-permute-start.14 = (f32[2,208,256]{2,1,0:T(8,128)S(1)}, f32[2,208,256]{2,1,0:T(8,128)S(1)}, u32[]{:S(2)}, u32[]{:S(2)}) collective-permute-start(f32[2,208,256]{2,1,0:T(8,128)S(1)} %collective-permute-done.13), channel_id=1, source_target_pairs={{0,2},{2,4},{4,6},{6,8},{8,10},{10,12},{12,14},{14,0},{1,3},{3,5},... | collective-permute-start | bytes 1277960 | tf_op jit(solution)/shard_map/ppermute | solution.py:27
  47.4 15.6 %copy-start.4 = (f32[2,208,256]{2,1,0:T(8,128)}, f32[2,208,256]{2,1,0:T(8,128)S(1)}, u32[]{:S(2)}) copy-start(f32[2,208,256]{2,1,0:T(8,128)S(1)} %collective-permute-done.4) | copy-start | bytes 1277956
  47.4 15.6 %collective-permute-start.5 = (f32[2,208,256]{2,1,0:T(8,128)S(1)}, f32[2,208,256]{2,1,0:T(8,128)S(1)}, u32[]{:S(2)}, u32[]{:S(2)}) collective-permute-start(f32[2,208,256]{2,1,0:T(8,128)S(1)} %collective-permute-done.4), channel_id=1, source_target_pairs={{0,2},{2,4},{4,6},{6,8},{8,10},{10,12},{12,14},{14,0},{1,3},{3,5},... | collective-permute-start | bytes 1277960 | tf_op jit(solution)/shard_map/ppermute | solution.py:27
  52.1 46.3 %copy-start.30 = (f32[2,16,256]{2,1,0:T(8,128)}, f32[2,16,256]{2,1,0:T(8,128)S(1)}, u32[]{:S(2)}) copy-start(f32[2,16,256]{2,1,0:T(8,128)S(1)} %slice.296) | copy-start | bytes 98308
  53.2 22.8 %copy-start.16 = (f32[2,208,256]{2,1,0:T(8,128)}, f32[2,208,256]{2,1,0:T(8,128)S(1)}, u32[]{:S(2)}) copy-start(f32[2,208,256]{2,1,0:T(8,128)S(1)} %collective-permute-done.2) | copy-start | bytes 1277956
  53.2 27.4 %copy-start.28 = (f32[2,16,256]{2,1,0:T(8,128)}, f32[2,16,256]{2,1,0:T(8,128)S(1)}, u32[]{:S(2)}) copy-start(f32[2,16,256]{2,1,0:T(8,128)S(1)} %slice.254) | copy-start | bytes 98308
  53.2 22.7 %collective-permute-start.3 = (f32[2,208,256]{2,1,0:T(8,128)S(1)}, f32[2,208,256]{2,1,0:T(8,128)S(1)}, u32[]{:S(2)}, u32[]{:S(2)}) collective-permute-start(f32[2,208,256]{2,1,0:T(8,128)S(1)} %collective-permute-done.2), channel_id=1, source_target_pairs={{0,14},{2,0},{4,2},{6,4},{8,6},{10,8},{12,10},{14,12},{1,15},{3,1}... | collective-permute-start | bytes 1277960 | tf_op jit(solution)/shard_map/ppermute | solution.py:31
  63.0 17.6 %copy-start.12 = (f32[2,208,256]{2,1,0:T(8,128)}, f32[2,208,256]{2,1,0:T(8,128)S(1)}, u32[]{:S(2)}) copy-start(f32[2,208,256]{2,1,0:T(8,128)S(1)} %collective-permute-done.5) | copy-start | bytes 1277956
  63.6 16.9 %collective-permute-start.6 = (f32[2,208,256]{2,1,0:T(8,128)S(1)}, f32[2,208,256]{2,1,0:T(8,128)S(1)}, u32[]{:S(2)}, u32[]{:S(2)}) collective-permute-start(f32[2,208,256]{2,1,0:T(8,128)S(1)} %collective-permute-done.5), channel_id=1, source_target_pairs={{0,2},{2,4},{4,6},{6,8},{8,10},{10,12},{12,14},{14,0},{1,3},{3,5},... | collective-permute-start | bytes 1277960 | tf_op jit(solution)/shard_map/ppermute | solution.py:27
  65.6 15.0 %copy-start.18 = (f32[2,208,256]{2,1,0:T(8,128)}, f32[2,208,256]{2,1,0:T(8,128)S(1)}, u32[]{:S(2)}) copy-start(f32[2,208,256]{2,1,0:T(8,128)S(1)} %collective-permute-done.11) | copy-start | bytes 1277956
  65.6 8.7 %copy-start.32 = (f32[2,16,256]{2,1,0:T(8,128)}, f32[2,16,256]{2,1,0:T(8,128)S(1)}, u32[]{:S(2)}) copy-start(f32[2,16,256]{2,1,0:T(8,128)S(1)} %slice.292) | copy-start | bytes 98308
  65.6 17.0 %collective-permute-start.12 = (f32[2,208,256]{2,1,0:T(8,128)S(1)}, f32[2,208,256]{2,1,0:T(8,128)S(1)}, u32[]{:S(2)}, u32[]{:S(2)}) collective-permute-start(f32[2,208,256]{2,1,0:T(8,128)S(1)} %collective-permute-done.11), channel_id=1, source_target_pairs={{0,14},{2,0},{4,2},{6,4},{8,6},{10,8},{12,10},{14,12},{1,15},{3,1}... | collective-permute-start | bytes 1277960 | tf_op jit(solution)/shard_map/ppermute | solution.py:31
  70.2 10.4 %copy-start.14 = (f32[2,208,256]{2,1,0:T(8,128)}, f32[2,208,256]{2,1,0:T(8,128)S(1)}, u32[]{:S(2)}) copy-start(f32[2,208,256]{2,1,0:T(8,128)S(1)} %collective-permute-done.14) | copy-start | bytes 1277956
  70.2 17.0 %collective-permute-start.15 = (f32[2,208,256]{2,1,0:T(8,128)S(1)}, f32[2,208,256]{2,1,0:T(8,128)S(1)}, u32[]{:S(2)}, u32[]{:S(2)}) collective-permute-start(f32[2,208,256]{2,1,0:T(8,128)S(1)} %collective-permute-done.14), channel_id=1, source_target_pairs={{0,2},{2,4},{4,6},{6,8},{8,10},{10,12},{12,14},{14,0},{1,3},{3,5},... | collective-permute-start | bytes 1277960 | tf_op jit(solution)/shard_map/ppermute | solution.py:27
  75.4 23.0 %copy-start.33 = (f32[2,16,256]{2,1,0:T(8,128)}, f32[2,16,256]{2,1,0:T(8,128)S(1)}, u32[]{:S(2)}) copy-start(f32[2,16,256]{2,1,0:T(8,128)S(1)} %slice.295) | copy-start | bytes 98308
  76.0 16.2 %collective-permute-start.8 = (f32[208,256]{1,0:T(8,128)S(1)}, f32[208,256]{1,0:T(8,128)S(1)}, u32[]{:S(2)}, u32[]{:S(2)}) collective-permute-start(f32[208,256]{1,0:T(8,128)S(1)} %slice_bitcast_fusion.2), channel_id=1, source_target_pairs={{0,14},{2,0},{4,2},{6,4},{8,6},{10,8},{12,10},{14,12},{1,15},{3,1}... | collective-permute-start | bytes 638984 | tf_op jit(solution)/shard_map/ppermute | solution.py:31
  80.6 16.7 %copy-start = (f32[2,208,256]{2,1,0:T(8,128)}, f32[2,208,256]{2,1,0:T(8,128)S(1)}, u32[]{:S(2)}) copy-start(f32[2,208,256]{2,1,0:T(8,128)S(1)} %collective-permute-done.6) | copy-start | bytes 1277956
  80.6 11.5 %collective-permute-start.7 = (f32[208,256]{1,0:T(8,128)S(1)}, f32[208,256]{1,0:T(8,128)S(1)}, u32[]{:S(2)}, u32[]{:S(2)}) collective-permute-start(f32[208,256]{1,0:T(8,128)S(1)} %slice_bitcast_fusion.3), channel_id=1, source_target_pairs={{0,2},{2,4},{4,6},{6,8},{8,10},{10,12},{12,14},{14,0},{1,3},{3,5},... | collective-permute-start | bytes 638984 | tf_op jit(solution)/shard_map/ppermute | solution.py:27
  82.6 9.6 %collective-permute-start.17 = (f32[208,256]{1,0:T(8,128)S(1)}, f32[208,256]{1,0:T(8,128)S(1)}, u32[]{:S(2)}, u32[]{:S(2)}) collective-permute-start(f32[208,256]{1,0:T(8,128)S(1)} %slice_bitcast_fusion), channel_id=1, source_target_pairs={{0,14},{2,0},{4,2},{6,4},{8,6},{10,8},{12,10},{14,12},{1,15},{3,1}... | collective-permute-start | bytes 638984 | tf_op jit(solution)/shard_map/ppermute | solution.py:31
  87.2 10.6 %copy-start.2 = (f32[2,208,256]{2,1,0:T(8,128)}, f32[2,208,256]{2,1,0:T(8,128)S(1)}, u32[]{:S(2)}) copy-start(f32[2,208,256]{2,1,0:T(8,128)S(1)} %collective-permute-done.15) | copy-start | bytes 1277956
  87.2 9.0 %collective-permute-start.16 = (f32[208,256]{1,0:T(8,128)S(1)}, f32[208,256]{1,0:T(8,128)S(1)}, u32[]{:S(2)}, u32[]{:S(2)}) collective-permute-start(f32[208,256]{1,0:T(8,128)S(1)} %slice_bitcast_fusion.1), channel_id=1, source_target_pairs={{0,2},{2,4},{4,6},{6,8},{8,10},{10,12},{12,14},{14,0},{1,3},{3,5},... | collective-permute-start | bytes 638984 | tf_op jit(solution)/shard_map/ppermute | solution.py:27
  89.3 8.4 %copy-start.31 = (f32[2,16,256]{2,1,0:T(8,128)}, f32[2,16,256]{2,1,0:T(8,128)S(1)}, u32[]{:S(2)}) copy-start(f32[2,16,256]{2,1,0:T(8,128)S(1)} %slice.255) | copy-start | bytes 98308
  90.0 7.8 %copy-start.35 = (f32[2,16,256]{2,1,0:T(8,128)}, f32[2,16,256]{2,1,0:T(8,128)S(1)}, u32[]{:S(2)}) copy-start(f32[2,16,256]{2,1,0:T(8,128)S(1)} %slice.293) | copy-start | bytes 98308
  90.0 8.4 %copy-start.34 = (f32[2,16,256]{2,1,0:T(8,128)}, f32[2,16,256]{2,1,0:T(8,128)S(1)}, u32[]{:S(2)}) copy-start(f32[2,16,256]{2,1,0:T(8,128)S(1)} %slice.294) | copy-start | bytes 98308
  92.2 6.2 %copy-start.20 = (f32[208,256]{1,0:T(8,128)}, f32[208,256]{1,0:T(8,128)S(1)}, u32[]{:S(2)}) copy-start(f32[208,256]{1,0:T(8,128)S(1)} %collective-permute-done.7) | copy-start | bytes 638980
  92.2 6.2 %copy-start.22 = (f32[208,256]{1,0:T(8,128)}, f32[208,256]{1,0:T(8,128)S(1)}, u32[]{:S(2)}) copy-start(f32[208,256]{1,0:T(8,128)S(1)} %collective-permute-done.17) | copy-start | bytes 638980
  96.2 2.8 %copy-start.26 = (f32[2,16,256]{2,1,0:T(8,128)}, f32[2,16,256]{2,1,0:T(8,128)S(1)}, u32[]{:S(2)}) copy-start(f32[2,16,256]{2,1,0:T(8,128)S(1)} %pad_maximum_fusion.7) | copy-start | bytes 98308
  100.4 35.8 %all-to-all-start = ((f32[16,64,128]{2,1,0:T(8,128)}), f32[16,64,128]{2,1,0:T(8,128)}, u32[]{:S(2)}, u32[]{:S(2)}) async-start(f32[16,64,128]{2,1,0:T(8,128)} %bitcast.258), calls=%async_computation | async-start | bytes 1048576 | tf_op jit(solution)/shard_map/all_to_all | solution.py:54
  137.9 4.9 %collective-permute-start.18 = (f32[64,128]{1,0:T(8,128)}, f32[64,128]{1,0:T(8,128)S(1)}, u32[]{:S(2)}, u32[]{:S(2)}) collective-permute-start(f32[64,128]{1,0:T(8,128)} %reduce_sum.9), channel_id=1, source_target_pairs={{0,256},{256,0},{1,257},{257,1},{2,258},{258,2},{3,259},{259,3},{4... | collective-permute-start | bytes 98312 | tf_op jit(solution)/shard_map/ppermute | solution.py:23
  144.3 21.5 %all-to-all-start.1 = ((f32[16,64,128]{2,1,0:T(8,128)}), f32[16,64,128]{2,1,0:T(8,128)}, u32[]{:S(2)}, u32[]{:S(2)}) async-start(f32[16,64,128]{2,1,0:T(8,128)} %broadcast_in_dim.2), calls=%async_computation.1 | async-start | bytes 1048576 | tf_op jit(solution)/shard_map/all_to_all | solution.py:59
  165.8 3.2 %copy-start.37 = (f32[512,256]{1,0:T(8,128)S(1)}, f32[512,256]{1,0:T(8,128)}, u32[]{:S(2)}) copy-start(f32[512,256]{1,0:T(8,128)} %constant_dynamic-update-slice_fusion.20) | copy-start | bytes 1572868
  165.8 3.5 %copy-start.23 = (f32[208,256]{1,0:T(8,128)S(1)}, f32[208,256]{1,0:T(8,128)}, u32[]{:S(2)}) copy-start(f32[208,256]{1,0:T(8,128)} %copy-done.22) | copy-start | bytes 638980
  165.8 3.5 %copy-start.25 = (f32[208,256]{1,0:T(8,128)S(1)}, f32[208,256]{1,0:T(8,128)}, u32[]{:S(2)}) copy-start(f32[208,256]{1,0:T(8,128)} %copy-done.24) | copy-start | bytes 638980
  165.8 4.5 %copy-start.19 = (f32[2,208,256]{2,1,0:T(8,128)S(1)}, f32[2,208,256]{2,1,0:T(8,128)}, u32[]{:S(2)}) copy-start(f32[2,208,256]{2,1,0:T(8,128)} %copy-done.18) | copy-start | bytes 1277956
  167.1 3.6 %copy-start.11 = (f32[2,208,256]{2,1,0:T(8,128)S(1)}, f32[2,208,256]{2,1,0:T(8,128)}, u32[]{:S(2)}) copy-start(f32[2,208,256]{2,1,0:T(8,128)} %copy-done.10) | copy-start | bytes 1277956
  (11 other events, 23.5 us)

commit v2 on v0

v2 whole, which is shorter than its diff:
```python
import functools

import jax
import jax.numpy as jnp
from jax import lax
from jax.experimental import pallas as pl
from jax.experimental.pallas import tpu as pltpu
from jax.sharding import Mesh
from jax.sharding import PartitionSpec as P

AXES = ("xl", "z", "core", "y", "xh")
SIZES = (2, 8, 2, 8, 2)
NY = 8
ROWS = 192
PLAIN = ((1,), (0,))
LIMIT = 60 * 1024 * 1024


def dot(left, right, dims):
    return lax.dot_general(
        left,
        right,
        (dims, ((), ())),
        precision=lax.Precision.HIGH,
        preferred_element_type=jnp.float32,
    )


def swap(value, axis):
    return lax.ppermute(value, axis, [(0, 1), (1, 0)])


def after(value, *earlier):
    return lax.optimization_barrier((value, *earlier))[0]


def split(value):
    high = value.astype(jnp.bfloat16)
    return high, (value - high.astype(jnp.float32)).astype(jnp.bfloat16)


def pack_kernel(core_ref, one_ref, two_ref, tri_one_ref, tri_two_ref, out_ref):
    out_ref[:ROWS, :256] = one_ref[...]
    out_ref[:ROWS, 256:] = two_ref[...]
    tri = jnp.where(core_ref[0] == 0, tri_one_ref[...], tri_two_ref[...])
    out_ref[ROWS:, :256] = tri[:8]
    out_ref[ROWS:, 256:] = tri[8:]


def pack(core, panel_one, panel_two, factor_one, factor_two):
    vmem = pl.BlockSpec(memory_space=pltpu.VMEM)
    return pl.pallas_call(
        pack_kernel,
        out_shape=jax.ShapeDtypeStruct((ROWS + 8, 512), jnp.float32),
        in_specs=[pl.BlockSpec(memory_space=pltpu.SMEM)] + [vmem] * 4,
        out_specs=vmem,
        name="pack",
    )(core, panel_one, panel_two, factor_one, factor_two)


def products_kernel(
    place_ref, near_ref, mine_ref, seen_ref, keep_ref, send_ref, inner, cross
):
    side, core = place_ref[0], place_ref[1]
    step = pl.program_id(0)
    count = near_ref.shape[0]
    left = near_ref[:, :ROWS, :].reshape(count * ROWS, 512)
    right = jnp.concatenate(
        [
            mine_ref[:, side].reshape(count * ROWS, 128),
            seen_ref[...].reshape(count * ROWS, 128),
        ],
        axis=1,
    )
    high, low = split(left)
    right_high, right_low = split(right)
    by_rows = (((0,), (0,)), ((), ()))

    def triple(a, a_low, b, b_low):
        return lax.dot_general(
            jnp.concatenate([a, a, a_low]),
            jnp.concatenate([b, b_low, b]),
            by_rows,
            preferred_element_type=jnp.float32,
        )

    inner_part = triple(high, low, right_high, right_low)
    cross_part = triple(high[:, :256], low[:, :256], high[:, 256:], low[:, 256:])
    inner_part = inner_part.reshape(2, 256, 256)
    cross_part = cross_part.reshape(2, 128, 256)

    @pl.when(step == 0)
    def _():
        inner[...] = inner_part
        cross[...] = cross_part

    @pl.when(step > 0)
    def _():
        inner[...] += inner_part
        cross[...] += cross_part

    @pl.when(step == pl.num_programs(0) - 1)
    def _():
        for out_ref, which in ((keep_ref, core), (send_ref, 1 - core)):
            out_ref[:256] = inner[which, :, :128]
            out_ref[256:512] = inner[which, :, 128:]
            out_ref[512:640] = cross[which, :, :128]
            out_ref[640:] = cross[which, :, 128:]


def products(place, near, by_owner, seen):
    count = 4
    return pl.pallas_call(
        products_kernel,
        grid=(NY // count,),
        out_shape=[jax.ShapeDtypeStruct((768, 128), jnp.float32)] * 2,
        in_specs=[
            pl.BlockSpec(memory_space=pltpu.SMEM),
            pl.BlockSpec((count, ROWS + 8, 512), lambda i: (i, 0, 0)),
            pl.BlockSpec((count, 2, ROWS, 128), lambda i: (i, 0, 0, 0)),
            pl.BlockSpec((count, ROWS, 128), lambda i: (i, 0, 0)),
        ],
        out_specs=[pl.BlockSpec((768, 128), lambda i: (0, 0))] * 2,
        scratch_shapes=[
            pltpu.VMEM((2, 256, 256), jnp.float32),
            pltpu.VMEM((2, 128, 256), jnp.float32),
        ],
        compiler_params=pltpu.CompilerParams(vmem_limit_bytes=LIMIT),
        name="products",
    )(place, near, by_owner, seen)


def update_kernel(place_ref, near_ref, far_ref, coeff_ref, old_ref, out_ref):
    side = place_ref[0]
    count = near_ref.shape[0]
    high, low = split(coeff_ref[...])
    both = jnp.concatenate([high, low], axis=1)
    for ref, which in ((near_ref, side), (far_ref, 1 - side)):
        panel = ref[:, :ROWS, :].reshape(count * ROWS, 512)
        panel_high, panel_low = split(panel)
        main = jnp.dot(panel_high, both, preferred_element_type=jnp.float32)
        rest = jnp.dot(panel_low, high, preferred_element_type=jnp.float32)
        change = main[:, :128] + (main[:, 128:] + rest)
        out_ref[:, which] = old_ref[:, which] - change.reshape(count, ROWS, 128)


def update(place, near, far, coeffs, by_owner):
    count = 2
    return pl.pallas_call(
        update_kernel,
        grid=(NY // count,),
        out_shape=jax.ShapeDtypeStruct(by_owner.shape, jnp.float32),
        in_specs=[
            pl.BlockSpec(memory_space=pltpu.SMEM),
            pl.BlockSpec((count, ROWS + 8, 512), lambda i: (i, 0, 0)),
            pl.BlockSpec((count, ROWS, 512), lambda i: (i, 0, 0)),
            pl.BlockSpec((512, 128), lambda i: (0, 0)),
            pl.BlockSpec((count, 2, ROWS, 128), lambda i: (i, 0, 0, 0)),
        ],
        out_specs=pl.BlockSpec((count, 2, ROWS, 128), lambda i: (i, 0, 0, 0)),
        compiler_params=pltpu.CompilerParams(vmem_limit_bytes=LIMIT),
        name="update",
    )(place, near, far, coeffs, by_owner)


def shards(vectors, panel_one, factor_one, panel_two, factor_two):
    side, core = lax.axis_index("xh"), lax.axis_index("core")
    place = jnp.stack([side, core]).astype(jnp.int32)

    own = pack(core[None], panel_one, panel_two, factor_one, factor_two)
    near = lax.all_gather(own, "y", axis=0)
    by_owner = vectors.reshape(NY, 2, ROWS, 128)
    theirs = lax.dynamic_index_in_dim(by_owner, 1 - side, 1, False)
    seen = swap(theirs, "xh")
    far = lax.all_gather(swap(own[:ROWS], "xh"), "y", axis=0)

    keep, send = products(place, near, by_owner, seen)
    part = keep + swap(send, "core")
    other = swap(part[256:], "xh")
    part = jnp.concatenate([part[:256] + other[:256], part[512:] + other[256:]])
    piece = lax.all_to_all(part.reshape(16, 32, 128), ("xl", "z"), 0, 0).sum(0)
    spread = jnp.broadcast_to(piece[None], (16, 32, 128))
    part = lax.all_to_all(spread, ("xl", "z"), 0, 0).reshape(512, 128)

    tri = near[:, ROWS:]
    tri = jnp.concatenate([tri[..., :256], tri[..., 256:]], axis=1)
    tri = lax.all_gather(tri, "core", axis=0)
    other = swap(tri, "xh")
    tri = jnp.where(
        side == 0,
        jnp.stack([tri, other], axis=2),
        jnp.stack([other, tri], axis=2),
    ).reshape(2, 256, 256)

    both = lax.all_gather(part, "core", axis=0)
    cross = jnp.concatenate([both[:, 256:384], both[:, 384:]], axis=2)
    inner_one, inner_two, cross = both[0, :256], both[1, :256], cross.reshape(256, 256)
    coeff_two = dot(tri[1], inner_two, PLAIN)
    coeff_one = dot(tri[0], inner_one - dot(cross, coeff_two, PLAIN), PLAIN)
    coeffs = jnp.concatenate([coeff_one, coeff_two])
    return update(place, near, far, coeffs, by_owner).reshape(vectors.shape)


def solution(mesh):
    fine = Mesh(mesh.devices.reshape(SIZES), AXES)
    prow, pcol = ("xl", "z", "core"), ("y", "xh")
    in_specs = (
        P(prow, pcol),
        P(prow + pcol, None),
        P(pcol, None),
        P(prow + pcol, None),
        P(pcol, None),
    )
    return jax.shard_map(
        shards,
        mesh=fine,
        in_specs=in_specs,
        out_specs=P(prow, pcol),
        check_vma=False,
    )
```

time: 648 us -> 138 us (0.21)
  waiting for transfers between devices: 544 us -> 56.7 us
  blocking collectives: 63.3 us -> 7.14 us
  starting transfers between devices: 0.12 us -> 38.1 us
  matrix products: 25.1 us -> 0.83 us
  Pallas kernels: 0 us -> 13.2 us
    psum x2 -> x0, waiting for transfers between devices: 348 us -> none  [combine(): return applier(lax.psum(partial_value, 'prow'))]
    all_gather x2, waiting for transfers between devices: 195 us -> 22.7 us  [the longest x1 22.7 us: shards(): near = lax.all_gather(own, 'y', axis=0)]
    all_gather x2, blocking collectives: 63.3 us -> 7.14 us  [the longest x1 4.13 us: shards(): both = lax.all_gather(part, 'core', axis=0)]
    ppermute x0 -> x5, waiting for transfers between devices: none -> 25.4 us  [swap(): return lax.ppermute(value, axis, [(0, 1), (1, 0)])]
    dot_general x6 -> x3, matrix products: 25.1 us -> 0.83 us  [dot(): lax.dot_general(left, right, (dims, ((), ())), precision=lax.Precision.HI...]
    ppermute x0 -> x5, starting transfers between devices: none -> 22.6 us  [swap(): return lax.ppermute(value, axis, [(0, 1), (1, 0)])]
    all_to_all x0 -> x2, starting transfers between devices: none -> 15.4 us  [the longest x1 8.21 us: shards(): piece = lax.all_to_all(part.reshape(16, 32, 128), ('xl', 'z'), 0, 0).sum(0)]
    pallas_call x0 -> x3, Pallas kernels: none -> 13.2 us  [the longest x1 6.23 us: update(): pl.pallas_call(update_kernel, grid=(NY // count,), out_shape=jax.ShapeDty...]
  transfers between devices with their start and end apart: 4 -> 9, of which waited for: 4 -> 6; matrix products, arithmetic and copies ran while one was open for 1% -> 6% of each run, Pallas kernels for 0% -> 4%
where the time goes in v2:
time: 138 us; the launch traced here: 137 us
  waiting for transfers between devices  56.7 us (41%)
  starting transfers between devices  38.1 us (28%)
  between operations  13.6 us (10%)
  Pallas kernels  13.2 us (10%)
  blocking collectives  7.14 us (5%)
  local copies, waits for them, and re-layouts  4.66 us (3%)
  other arithmetic  3.29 us (2%)
    ppermute x5, waiting for transfers between devices, swap(): return lax.ppermute(value, axis, [(0, 1), (1, 0)])  25.4 us
    all_gather x1, waiting for transfers between devices, shards(): near = lax.all_gather(own, 'y', axis=0)  22.7 us
    ppermute x5, starting transfers between devices, swap(): return lax.ppermute(value, axis, [(0, 1), (1, 0)])  22.6 us
    all_to_all x1, waiting for transfers between devices, shards(): part = lax.all_to_all(spread, ('xl', 'z'), 0, 0).reshape(512, 128)  8.63 us
    all_to_all x1, starting transfers between devices, shards(): piece = lax.all_to_all(part.reshape(16, 32, 128), ('xl', 'z'), 0, 0).sum(0)  8.21 us
    all_to_all x1, starting transfers between devices, shards(): part = lax.all_to_all(spread, ('xl', 'z'), 0, 0).reshape(512, 128)  7.23 us
    pallas_call x1, Pallas kernels, update(): pl.pallas_call(update_kernel, grid=(NY // count,), out_shape=jax.ShapeDty...  6.23 us
    pallas_call x1, Pallas kernels, products(): pl.pallas_call(products_kernel, grid=(NY // count,), out_shape=[jax.Shape...  5.11 us
  transfers between devices with their start and end apart: 9, of which 6 were waited for; matrix products, arithmetic and copies ran while one was open for 6% of the time, Pallas kernels for 4%

profile of v2, /device:TPU:1, one launch (start us, length us, event | category | flops | bytes accessed | tf_op | source)
XLA Modules:
  0.0 137.5 jit_solution(10688582637955987870)
XLA Ops:
  6.5 0.0 all-gather.6.cloned.1.call-start
  6.5 1.8 %pack.1 = f32[200,512]{1,0:T(8,128)} custom-call(s32[1]{0:T(128)} %bitcast.1.core_ref, f32[192,256]{1,0:T(8,128)} %one_ref.1, f32[192,256]{1,0:T(8,128)} %two_ref.1, f32[16,256]{1,0:T(8,128)} %tri_one_ref.1, f32[16,256]{1,0:T(8,128)} %tri_two_ref.1), custom_call_target="tpu_custom_call" | custom-call | tf_op jit(solution)/shard_map/pack/pallas_call | solution.py:52
  8.4 0.0 all-gather.6.cloned.1.call-update
  8.4 0.0 all-gather.8.cloned.1.call-start
  8.4 1.0 slice.61
  9.5 5.5 %collective-permute-start = (f32[192,512]{1,0:T(8,128)S(1)}, f32[192,512]{1,0:T(8,128)S(1)}, u32[]{:S(2)}, u32[]{:S(2)}) collective-permute-start(f32[192,512]{1,0:T(8,128)S(1)} %slice.61), channel_id=1, source_target_pairs={{0,1},{1,0},{2,3},{3,2},{4,5},{5,4},{6,7},{7,6},{8,9},{9,8},{10,11... | collective-permute-start | bytes 1179656 | tf_op jit(solution)/shard_map/ppermute | solution.py:30
  14.9 5.3 %collective-permute-done = f32[192,512]{1,0:T(8,128)S(1)} collective-permute-done((f32[192,512]{1,0:T(8,128)S(1)}, f32[192,512]{1,0:T(8,128)S(1)}, u32[]{:S(2)}, u32[]{:S(2)}) %collective-permute-start) | collective-permute-done | bytes 393248 | tf_op jit(solution)/shard_map/ppermute | solution.py:30
  20.3 0.0 copy-start.1
  20.3 0.8 copy-done.1
  21.0 0.0 all-gather.8.cloned.1.call-update
  21.1 1.2 dynamic-slice_bitcast_fusion
  22.3 5.6 %collective-permute-start.2 = (f32[8,192,128]{2,1,0:T(8,128)S(1)}, f32[8,192,128]{2,1,0:T(8,128)S(1)}, u32[]{:S(2)}, u32[]{:S(2)}) collective-permute-start(f32[8,192,128]{2,1,0:T(8,128)S(1)} %dynamic-slice_bitcast_fusion), channel_id=1, source_target_pairs={{0,1},{1,0},{2,3},{3,2},{4,5},{5,4},{6,7},{7,6},{8,9},{9,8},{10,11... | collective-permute-start | bytes 2359304 | tf_op jit(solution)/shard_map/ppermute | solution.py:30
  27.9 0.7 pad_add_fusion.place_ref
  28.6 12.2 %collective-permute-done.2.seen_ref = f32[8,192,128]{2,1,0:T(8,128)S(1)} collective-permute-done((f32[8,192,128]{2,1,0:T(8,128)S(1)}, f32[8,192,128]{2,1,0:T(8,128)S(1)}, u32[]{:S(2)}, u32[]{:S(2)}) %collective-permute-start.2) | collective-permute-done | bytes 786464 | tf_op jit(solution)/shard_map/ppermute | solution.py:30
  40.7 0.0 copy-start
  40.7 22.7 %all-gather.6.cloned.1.call-done = f32[1600,512]{1,0:T(8,128)} async-done(((f32[200,512]{1,0:T(8,128)}), f32[1600,512]{1,0:T(8,128)}) %all-gather.6.cloned.1.call-update) | async-done | bytes 3276816 | tf_op jit(solution)/shard_map/all_gather | solution.py:171
  63.4 0.0 copy-done
  63.4 5.1 %products.1 = (f32[768,128]{1,0:T(8,128)}, f32[768,128]{1,0:T(8,128)}) custom-call(s32[2]{0:T(128)} %pad_add_fusion.place_ref, f32[8,200,512]{2,1,0:T(8,128)} %bitcast.28, f32[8,2,192,128]{3,2,1,0:T(8,128)} %bitcast.32, f32[8,192,128]{2,1,0:T(8,128)} %copy-done), custom_call_target="tpu_custom_call" | custom-call | tf_op jit(solution)/shard_map/products/pallas_call | solution.py:113
  68.6 2.6 %collective-permute-start.3 = (f32[768,128]{1,0:T(8,128)}, f32[768,128]{1,0:T(8,128)S(1)}, u32[]{:S(2)}, u32[]{:S(2)}) collective-permute-start(f32[768,128]{1,0:T(8,128)} %get-tuple-element.8), channel_id=1, source_target_pairs={{0,16},{16,0},{1,17},{17,1},{2,18},{18,2},{3,19},{19,3},{4,20},{20... | collective-permute-start | bytes 1179656 | tf_op jit(solution)/shard_map/ppermute | solution.py:30
  71.2 1.5 %collective-permute-done.3 = f32[768,128]{1,0:T(8,128)S(1)} collective-permute-done((f32[768,128]{1,0:T(8,128)}, f32[768,128]{1,0:T(8,128)S(1)}, u32[]{:S(2)}, u32[]{:S(2)}) %collective-permute-start.3) | collective-permute-done | bytes 393248 | tf_op jit(solution)/shard_map/ppermute | solution.py:30
  72.7 1.1 add.15
  73.8 4.6 %collective-permute-start.4 = (f32[512,128]{1,0:T(8,128)S(1)}, f32[512,128]{1,0:T(8,128)S(1)}, u32[]{:S(2)}, u32[]{:S(2)}) collective-permute-start(f32[512,128]{1,0:T(8,128)S(1)} %slice.66), channel_id=1, source_target_pairs={{0,1},{1,0},{2,3},{3,2},{4,5},{5,4},{6,7},{7,6},{8,9},{9,8},{10,11... | collective-permute-start | bytes 786440 | tf_op jit(solution)/shard_map/ppermute | solution.py:30
  78.4 6.3 %collective-permute-done.4 = f32[512,128]{1,0:T(8,128)S(1)} collective-permute-done((f32[512,128]{1,0:T(8,128)S(1)}, f32[512,128]{1,0:T(8,128)S(1)}, u32[]{:S(2)}, u32[]{:S(2)}) %collective-permute-start.4) | collective-permute-done | bytes 262176 | tf_op jit(solution)/shard_map/ppermute | solution.py:30
  84.8 0.7 pad_maximum_fusion
  85.5 8.2 %all-to-all-start = ((f32[16,32,128]{2,1,0:T(8,128)}), f32[16,32,128]{2,1,0:T(8,128)S(1)}, u32[]{:S(2)}, u32[]{:S(2)}) async-start(f32[16,32,128]{2,1,0:T(8,128)} %bitcast.10), calls=%async_computation | async-start | bytes 524288 | tf_op jit(solution)/shard_map/all_to_all | solution.py:181
  93.7 0.9 fusion.1
  94.6 3.0 %all-gather.2 = f32[16,16,256]{2,1,0:T(8,128)S(1)} all-gather(f32[8,16,256]{2,1,0:T(8,128)S(1)} %pad_maximum_fusion.3), channel_id=4, replica_groups=mesh['xl'=2,'z'=8,'core'=2,'y'=8,'xh'=2] {'core'}, dimensions={0}, use_global_device_ids=true | all-gather | bytes 393216 | tf_op jit(solution)/shard_map/all_gather | solution.py:187
  97.6 4.3 %collective-permute-start.1 = (f32[2,8,16,256]{3,2,1,0:T(8,128)S(1)}, f32[2,8,16,256]{3,2,1,0:T(8,128)S(1)}, u32[]{:S(2)}, u32[]{:S(2)}) collective-permute-start(f32[2,8,16,256]{3,2,1,0:T(8,128)S(1)} %bitcast.37), channel_id=1, source_target_pairs={{0,1},{1,0},{2,3},{3,2},{4,5},{5,4},{6,7},{7,6},{8,9},{9,8},{10,11... | collective-permute-start | bytes 786440 | tf_op jit(solution)/shard_map/ppermute | solution.py:30
  101.9 0.0 all-to-all-done
  102.0 0.7 broadcast_in_dim.2
  102.7 7.2 %all-to-all-start.1 = ((f32[16,32,128]{2,1,0:T(8,128)}), f32[16,32,128]{2,1,0:T(8,128)S(1)}, u32[]{:S(2)}, u32[]{:S(2)}) async-start(f32[16,32,128]{2,1,0:T(8,128)} %broadcast_in_dim.2), calls=%async_computation.1 | async-start | bytes 524288 | tf_op jit(solution)/shard_map/all_to_all | solution.py:183
  109.9 0.0 collective-permute-done.1
  110.0 8.6 %all-to-all-done.1 = f32[16,32,128]{2,1,0:T(8,128)S(1)} async-done(((f32[16,32,128]{2,1,0:T(8,128)}), f32[16,32,128]{2,1,0:T(8,128)S(1)}, u32[]{:S(2)}, u32[]{:S(2)}) %all-to-all-start.1) | async-done | bytes 262176 | tf_op jit(solution)/shard_map/all_to_all | solution.py:183
  118.7 4.1 %all_gather.27 = f32[2,512,128]{2,1,0:T(8,128)S(1)} all-gather(f32[1,512,128]{2,1,0:T(8,128)S(1)} %bitcast.35), channel_id=1, replica_groups=mesh['xl'=2,'z'=8,'core'=2,'y'=8,'xh'=2] {'core'}, dimensions={0}, use_global_device_ids=true | all-gather | bytes 786432 | tf_op jit(solution)/shard_map/all_gather | solution.py:195
  122.8 0.3 fusion
  123.1 0.3 convolution_subtract_fusion
  123.4 0.3 fusion.4
  123.7 0.7 pad_maximum_fusion.2.coeff_ref
  124.4 0.0 all-gather.8.cloned.1.call-done
  124.4 6.2 %update.1 = f32[8,2,192,128]{3,2,1,0:T(8,128)} custom-call(s32[2]{0:T(128)} %pad_add_fusion.place_ref, f32[8,200,512]{2,1,0:T(8,128)} %bitcast.30, f32[8,192,512]{2,1,0:T(8,128)} %bitcast.34, f32[512,128]{1,0:T(8,128)} %pad_maximum_fusion.2.coeff_ref, f32[8,2,192,128]{3,2,1,0:T(8,128)} %bitcast.33), custom_call_target="tpu_custom_call" | custom-call | tf_op jit(solution)/shard_map/update/pallas_call | solution.py:149
  (8 shorter events, 0.2 us)
Async XLA Ops:
  6.5 56.9 %all-gather.6.cloned.1.call-start = ((), (), s32[]{:S(2)}) async-start(), calls=%async_computation.2 | async-start | bytes 3686400 | tf_op jit(solution)/shard_map/all_gather | solution.py:171
  8.4 116.0 %all-gather.8.cloned.1.call-start = ((), (), s32[]{:S(2)}) async-start(), calls=%async_computation.3 | async-start | bytes 3538944 | tf_op jit(solution)/shard_map/all_gather | solution.py:175
  9.5 10.8 %collective-permute-start = (f32[192,512]{1,0:T(8,128)S(1)}, f32[192,512]{1,0:T(8,128)S(1)}, u32[]{:S(2)}, u32[]{:S(2)}) collective-permute-start(f32[192,512]{1,0:T(8,128)S(1)} %slice.61), channel_id=1, source_target_pairs={{0,1},{1,0},{2,3},{3,2},{4,5},{5,4},{6,7},{7,6},{8,9},{9,8},{10,11... | collective-permute-start | bytes 1179656 | tf_op jit(solution)/shard_map/ppermute | solution.py:30
  20.3 0.8 copy-start.1
  22.3 18.5 %collective-permute-start.2 = (f32[8,192,128]{2,1,0:T(8,128)S(1)}, f32[8,192,128]{2,1,0:T(8,128)S(1)}, u32[]{:S(2)}, u32[]{:S(2)}) collective-permute-start(f32[8,192,128]{2,1,0:T(8,128)S(1)} %dynamic-slice_bitcast_fusion), channel_id=1, source_target_pairs={{0,1},{1,0},{2,3},{3,2},{4,5},{5,4},{6,7},{7,6},{8,9},{9,8},{10,11... | collective-permute-start | bytes 2359304 | tf_op jit(solution)/shard_map/ppermute | solution.py:30
  40.7 22.7 %copy-start = (f32[8,192,128]{2,1,0:T(8,128)}, f32[8,192,128]{2,1,0:T(8,128)S(1)}, u32[]{:S(2)}) copy-start(f32[8,192,128]{2,1,0:T(8,128)S(1)} %collective-permute-done.2.seen_ref) | copy-start | bytes 2359300
  68.6 4.2 %collective-permute-start.3 = (f32[768,128]{1,0:T(8,128)}, f32[768,128]{1,0:T(8,128)S(1)}, u32[]{:S(2)}, u32[]{:S(2)}) collective-permute-start(f32[768,128]{1,0:T(8,128)} %get-tuple-element.8), channel_id=1, source_target_pairs={{0,16},{16,0},{1,17},{17,1},{2,18},{18,2},{3,19},{19,3},{4,20},{20... | collective-permute-start | bytes 1179656 | tf_op jit(solution)/shard_map/ppermute | solution.py:30
  73.8 10.9 %collective-permute-start.4 = (f32[512,128]{1,0:T(8,128)S(1)}, f32[512,128]{1,0:T(8,128)S(1)}, u32[]{:S(2)}, u32[]{:S(2)}) collective-permute-start(f32[512,128]{1,0:T(8,128)S(1)} %slice.66), channel_id=1, source_target_pairs={{0,1},{1,0},{2,3},{3,2},{4,5},{5,4},{6,7},{7,6},{8,9},{9,8},{10,11... | collective-permute-start | bytes 786440 | tf_op jit(solution)/shard_map/ppermute | solution.py:30
  85.5 16.4 %all-to-all-start = ((f32[16,32,128]{2,1,0:T(8,128)}), f32[16,32,128]{2,1,0:T(8,128)S(1)}, u32[]{:S(2)}, u32[]{:S(2)}) async-start(f32[16,32,128]{2,1,0:T(8,128)} %bitcast.10), calls=%async_computation | async-start | bytes 524288 | tf_op jit(solution)/shard_map/all_to_all | solution.py:181
  97.6 12.3 %collective-permute-start.1 = (f32[2,8,16,256]{3,2,1,0:T(8,128)S(1)}, f32[2,8,16,256]{3,2,1,0:T(8,128)S(1)}, u32[]{:S(2)}, u32[]{:S(2)}) collective-permute-start(f32[2,8,16,256]{3,2,1,0:T(8,128)S(1)} %bitcast.37), channel_id=1, source_target_pairs={{0,1},{1,0},{2,3},{3,2},{4,5},{5,4},{6,7},{7,6},{8,9},{9,8},{10,11... | collective-permute-start | bytes 786440 | tf_op jit(solution)/shard_map/ppermute | solution.py:30
  102.7 16.0 %all-to-all-start.1 = ((f32[16,32,128]{2,1,0:T(8,128)}), f32[16,32,128]{2,1,0:T(8,128)S(1)}, u32[]{:S(2)}, u32[]{:S(2)}) async-start(f32[16,32,128]{2,1,0:T(8,128)} %broadcast_in_dim.2), calls=%async_computation.1 | async-start | bytes 524288 | tf_op jit(solution)/shard_map/all_to_all | solution.py:183
Sparse Core Ops, SparseCore 0:
  9.4 53.9 all-gather.5
  65.5 45.9 all-gather.7

commit v3 on v2

v3 whole, which is shorter than its diff:
```python
import functools

import jax
import jax.numpy as jnp
from jax import lax
from jax.experimental import pallas as pl
from jax.experimental.pallas import tpu as pltpu
from jax.sharding import Mesh
from jax.sharding import PartitionSpec as P

AXES = ("xl", "z", "core", "y", "xh")
SIZES = (2, 8, 2, 8, 2)
NY = 8
ROWS = 192
MIB = 1024 * 1024


def swap(value, axis):
    return lax.ppermute(value, axis, [(0, 1), (1, 0)])


def split(value):
    high = value.astype(jnp.bfloat16)
    return high, (value - high.astype(jnp.float32)).astype(jnp.bfloat16)


def pack_kernel(one_ref, two_ref, tri_one_ref, tri_two_ref, out_ref):
    out_ref[:ROWS, :256] = one_ref[...]
    out_ref[:ROWS, 256:] = two_ref[...]
    for i, ref in enumerate((tri_one_ref, tri_two_ref)):
        at = pl.ds(ROWS + 8 * i, 8)
        out_ref[at, :256] = ref[:8]
        out_ref[at, 256:] = ref[8:]


def pack(panel_one, panel_two, factor_one, factor_two):
    vmem = pl.BlockSpec(memory_space=pltpu.VMEM)
    return pl.pallas_call(
        pack_kernel,
        out_shape=jax.ShapeDtypeStruct((ROWS + 16, 512), jnp.float32),
        in_specs=[vmem] * 4,
        out_specs=vmem,
        name="pack",
    )(panel_one, panel_two, factor_one, factor_two)


def products_kernel(
    place_ref, near_ref, mine_ref, seen_ref, keep_ref, send_ref, inner, cross
):
    side, core = place_ref[0], place_ref[1]
    step = pl.program_id(0)
    count = near_ref.shape[0]
    left = near_ref[:, :ROWS, :].reshape(count * ROWS, 512)
    right = jnp.concatenate(
        [
            mine_ref[:, side].reshape(count * ROWS, 128),
            seen_ref[...].reshape(count * ROWS, 128),
        ],
        axis=1,
    )
    high, low = split(left)
    right_high, right_low = split(right)
    by_rows = (((0,), (0,)), ((), ()))

    def triple(a, a_low, b, b_low):
        return lax.dot_general(
            jnp.concatenate([a, a, a_low]),
            jnp.concatenate([b, b_low, b]),
            by_rows,
            preferred_element_type=jnp.float32,
        )

    inner_part = triple(high, low, right_high, right_low)
    cross_part = triple(high[:, :256], low[:, :256], high[:, 256:], low[:, 256:])
    inner_part = inner_part.reshape(2, 256, 256)
    cross_part = cross_part.reshape(2, 128, 256)

    @pl.when(step == 0)
    def _():
        inner[...] = inner_part
        cross[...] = cross_part

    @pl.when(step > 0)
    def _():
        inner[...] += inner_part
        cross[...] += cross_part

    @pl.when(step == pl.num_programs(0) - 1)
    def _():
        for out_ref, which in ((keep_ref, core), (send_ref, 1 - core)):
            own, far = inner[which, :, :128], inner[which, :, 128:]
            out_ref[:256] = jnp.where(side == 0, own, far)
            out_ref[256:512] = jnp.where(side == 0, far, own)
            out_ref[512:640] = cross[which, :, :128]
            out_ref[640:] = cross[which, :, 128:]


def products(place, near, by_owner, seen):
    count = 4
    return pl.pallas_call(
        products_kernel,
        grid=(NY // count,),
        out_shape=[jax.ShapeDtypeStruct((768, 128), jnp.float32)] * 2,
        in_specs=[
            pl.BlockSpec(memory_space=pltpu.SMEM),
            pl.BlockSpec((count, ROWS + 16, 512), lambda i: (i, 0, 0)),
            pl.BlockSpec((count, 2, ROWS, 128), lambda i: (i, 0, 0, 0)),
            pl.BlockSpec((count, ROWS, 128), lambda i: (i, 0, 0)),
        ],
        out_specs=[pl.BlockSpec((768, 128), lambda i: (0, 0))] * 2,
        scratch_shapes=[
            pltpu.VMEM((2, 256, 256), jnp.float32),
            pltpu.VMEM((2, 128, 256), jnp.float32),
        ],
        compiler_params=pltpu.CompilerParams(vmem_limit_bytes=48 * MIB),
        name="products",
    )(place, near, by_owner, seen)


def triple(left, right):
    (high, low), (right_high, right_low) = left, right
    both = jnp.concatenate([right_high, right_low], axis=1)
    main = jnp.dot(high, both, preferred_element_type=jnp.float32)
    rest = jnp.dot(low, right_high, preferred_element_type=jnp.float32)
    return main[:, :128] + (main[:, 128:] + rest)


def update_kernel(
    place_ref, near_ref, far_ref, sums_ref, near_tri_ref, far_tri_ref, old_ref,
    out_ref, coeffs, tri,
):
    side = place_ref[0]
    count = near_ref.shape[0]

    @pl.when(pl.program_id(0) == 0)
    def _():
        cross = jnp.concatenate(
            [
                jnp.concatenate([sums_ref[h, 256:384], sums_ref[h, 384:]], axis=1)
                for h in range(2)
            ]
        )
        for ref, which in ((near_tri_ref, side), (far_tri_ref, 1 - side)):
            for i in range(2):
                for j in range(2):
                    tri[i, :, which, pl.ds(8 * j, 8), :] = ref[
                        :, pl.ds(8 * i, 8), pl.ds(256 * j, 256)
                    ]
        tri_one, tri_two = (split(tri[i].reshape(256, 256)) for i in range(2))
        coeff_two = triple(tri_two, split(sums_ref[1, :256]))
        moved = sums_ref[0, :256] - triple(split(cross), split(coeff_two))
        coeffs[:256] = triple(tri_one, split(moved))
        coeffs[256:] = coeff_two

    right = split(coeffs[...])
    for ref, which in ((near_ref, side), (far_ref, 1 - side)):
        panel = ref[:, :ROWS, :].reshape(count * ROWS, 512)
        change = triple(split(panel), right).reshape(count, ROWS, 128)
        out_ref[:, which] = old_ref[:, which] - change


def update(place, near, far, sums, by_owner):
    count = 4
    return pl.pallas_call(
        update_kernel,
        grid=(NY // count,),
        out_shape=jax.ShapeDtypeStruct(by_owner.shape, jnp.float32),
        in_specs=[
            pl.BlockSpec(memory_space=pltpu.SMEM),
            pl.BlockSpec((count, ROWS + 16, 512), lambda i: (i, 0, 0)),
            pl.BlockSpec((count, ROWS + 16, 512), lambda i: (i, 0, 0)),
            pl.BlockSpec((2, 512, 128), lambda i: (0, 0, 0)),
            pl.BlockSpec((NY, 16, 512), lambda i: (0, ROWS // 16, 0)),
            pl.BlockSpec((NY, 16, 512), lambda i: (0, ROWS // 16, 0)),
            pl.BlockSpec((count, 2, ROWS, 128), lambda i: (i, 0, 0, 0)),
        ],
        out_specs=pl.BlockSpec((count, 2, ROWS, 128), lambda i: (i, 0, 0, 0)),
        scratch_shapes=[
            pltpu.VMEM((512, 128), jnp.float32),
            pltpu.VMEM((2, NY, 2, 16, 256), jnp.float32),
        ],
        compiler_params=pltpu.CompilerParams(vmem_limit_bytes=60 * MIB),
        name="update",
    )(place, near, far, sums, near, far, by_owner)


def shards(vectors, panel_one, factor_one, panel_two, factor_two):
    side, core = lax.axis_index("xh"), lax.axis_index("core")
    place = jnp.stack([side, core]).astype(jnp.int32)

    own = pack(panel_one, panel_two, factor_one, factor_two)
    near = lax.all_gather(own, "y", axis=0)
    by_owner = vectors.reshape(NY, 2, ROWS, 128)
    theirs = lax.dynamic_index_in_dim(by_owner, 1 - side, 1, False)
    seen = swap(theirs, "xh")
    far = lax.all_gather(swap(own, "xh"), "y", axis=0)

    keep, send = products(place, near, by_owner, seen)
    part = keep + swap(send, "core")
    inner = part[:512].reshape(2, 16, 16, 128).transpose(1, 0, 2, 3)
    cross = jnp.broadcast_to(part[512:].reshape(16, 1, 16, 128), (16, 2, 16, 128))
    parts = jnp.concatenate([inner, cross], axis=2).reshape(32, 32, 128)
    parts = lax.all_to_all(parts, ("xl", "z", "xh"), 0, 0)
    spread = jnp.broadcast_to(parts.sum(0)[None], (16, 32, 128))
    part = lax.all_to_all(spread, ("xl", "z"), 0, 0)
    part = part.reshape(16, 2, 16, 128).transpose(1, 0, 2, 3).reshape(512, 128)
    sums = lax.all_gather(part, "core", axis=0)
    return update(place, near, far, sums, by_owner).reshape(vectors.shape)


def solution(mesh):
    fine = Mesh(mesh.devices.reshape(SIZES), AXES)
    prow, pcol = ("xl", "z", "core"), ("y", "xh")
    in_specs = (
        P(prow, pcol),
        P(prow + pcol, None),
        P(pcol, None),
        P(prow + pcol, None),
        P(pcol, None),
    )
    return jax.shard_map(
        shards,
        mesh=fine,
        in_specs=in_specs,
        out_specs=P(prow, pcol),
        check_vma=False,
    )
```

time: 138 us -> 130 us (0.942)
  blocking collectives: 7.14 us -> 43.7 us
  starting transfers between devices: 38.1 us -> 13.6 us
  waiting for transfers between devices: 56.7 us -> 45.6 us
  local copies, waits for them, and re-layouts: 4.66 us -> 0.91 us
  other arithmetic: 3.29 us -> 0.22 us
    all_to_all x0 -> x2, blocking collectives: none -> 38.5 us  [the longest x1 25.8 us: shards(): parts = lax.all_to_all(parts, ('xl', 'z', 'xh'), 0, 0)]
    all_to_all x2 -> x0, starting transfers between devices: 15.4 us -> none  [the longest x1 8.21 us: shards(): piece = lax.all_to_all(part.reshape(16, 32, 128), ('xl', 'z'), 0, 0).sum(0)]
    ppermute x5 -> x3, starting transfers between devices: 22.6 us -> 13.6 us  [swap(): return lax.ppermute(value, axis, [(0, 1), (1, 0)])]
    all_to_all x2 -> x0, waiting for transfers between devices: 8.63 us -> none  [the longest x1 8.63 us: shards(): part = lax.all_to_all(spread, ('xl', 'z'), 0, 0).reshape(512, 128)]
    ppermute x5 -> x3, waiting for transfers between devices: 25.4 us -> 20.5 us  [swap(): return lax.ppermute(value, axis, [(0, 1), (1, 0)])]
    all_gather x1, waiting for transfers between devices: 22.7 us -> 25.1 us  [shards(): near = lax.all_gather(own, 'y', axis=0)]
    slice x5 -> x2, local copies, waits for them, and re-layouts: 1.98 us -> 0.03 us  [the longest x1 0.02 us: shards(): inner = part[:512].reshape(2, 16, 16, 128).transpose(1, 0, 2, 3)]
    all_gather x2 -> x1, blocking collectives: 7.14 us -> 5.25 us  [shards(): sums = lax.all_gather(part, 'core', axis=0)]
  transfers between devices with their start and end apart: 9 -> 5, of which waited for: 6 -> 4; matrix products, arithmetic and copies ran while one was open for 6% -> 0% of each run, Pallas kernels for 4% -> 3%
where the time goes in v3:
time: 130 us
  waiting for transfers between devices  45.6 us (35%)
  blocking collectives  43.7 us (34%)
  starting transfers between devices  13.6 us (10%)
  between operations  13.5 us (10%)
  Pallas kernels  12 us (9%)
    all_to_all x1, blocking collectives, shards(): parts = lax.all_to_all(parts, ('xl', 'z', 'xh'), 0, 0)  25.8 us
    all_gather x1, waiting for transfers between devices, shards(): near = lax.all_gather(own, 'y', axis=0)  25.1 us
    ppermute x3, waiting for transfers between devices, swap(): return lax.ppermute(value, axis, [(0, 1), (1, 0)])  20.5 us
    ppermute x3, starting transfers between devices, swap(): return lax.ppermute(value, axis, [(0, 1), (1, 0)])  13.6 us
    all_to_all x1, blocking collectives, shards(): part = lax.all_to_all(spread, ('xl', 'z'), 0, 0)  12.7 us
    pallas_call x1, Pallas kernels, update(): pl.pallas_call(update_kernel, grid=(NY // count,), out_shape=jax.ShapeDty...  6.08 us
    all_gather x1, blocking collectives, shards(): sums = lax.all_gather(part, 'core', axis=0)  5.25 us
    pallas_call x1, Pallas kernels, products(): pl.pallas_call(products_kernel, grid=(NY // count,), out_shape=[jax.Shape...  3.98 us
  transfers between devices with their start and end apart: 5, of which 4 were waited for; matrix products, arithmetic and copies ran while one was open for 0% of the time, Pallas kernels for 3%

profile of v3, /device:TPU:1, one launch (start us, length us, event | category | flops | bytes accessed | tf_op | source)
XLA Modules:
  0.0 129.6 jit_solution(9629236686200749233)
XLA Ops:
  6.5 0.0 copy-start
  6.5 0.0 all-gather.5.cloned.1.call-start
  6.5 1.9 %pack.1 = f32[208,512]{1,0:T(8,128)} custom-call(f32[192,256]{1,0:T(8,128)} %one_ref.1, f32[192,256]{1,0:T(8,128)} %two_ref.1, f32[16,256]{1,0:T(8,128)} %tri_one_ref.1, f32[16,256]{1,0:T(8,128)} %tri_two_ref.1), custom_call_target="tpu_custom_call" | custom-call | tf_op jit(solution)/shard_map/pack/pallas_call | solution.py:38
  8.5 0.0 all-gather.5.cloned.1.call-update
  8.5 0.0 all-gather.7.cloned.1.call-start
  8.5 5.5 %collective-permute-start = (f32[208,512]{1,0:T(8,128)}, f32[208,512]{1,0:T(8,128)S(1)}, u32[]{:S(2)}, u32[]{:S(2)}) collective-permute-start(f32[208,512]{1,0:T(8,128)} %pack.1), channel_id=1, source_target_pairs={{0,1},{1,0},{2,3},{3,2},{4,5},{5,4},{6,7},{7,6},{8,9},{9,8},{10,11... | collective-permute-start | bytes 1277960 | tf_op jit(solution)/shard_map/ppermute | solution.py:19
  14.0 6.4 %collective-permute-done = f32[208,512]{1,0:T(8,128)S(1)} collective-permute-done((f32[208,512]{1,0:T(8,128)}, f32[208,512]{1,0:T(8,128)S(1)}, u32[]{:S(2)}, u32[]{:S(2)}) %collective-permute-start) | collective-permute-done | bytes 426016 | tf_op jit(solution)/shard_map/ppermute | solution.py:19
  20.4 0.0 copy-start.2
  20.4 0.7 copy-done.2
  21.1 0.0 all-gather.7.cloned.1.call-update
  21.2 0.0 copy-done
  21.2 0.1 dynamic-slice_bitcast_fusion
  21.2 5.5 %collective-permute-start.1 = (f32[8,192,128]{2,1,0:T(8,128)S(1)}, f32[8,192,128]{2,1,0:T(8,128)S(1)}, u32[]{:S(2)}, u32[]{:S(2)}) collective-permute-start(f32[8,192,128]{2,1,0:T(8,128)S(1)} %dynamic-slice_bitcast_fusion), channel_id=1, source_target_pairs={{0,1},{1,0},{2,3},{3,2},{4,5},{5,4},{6,7},{7,6},{8,9},{9,8},{10,11... | collective-permute-start | bytes 2359304 | tf_op jit(solution)/shard_map/ppermute | solution.py:19
  26.8 0.1 pad_add_fusion.place_ref
  26.8 0.0 copy-start.1
  26.8 12.8 %collective-permute-done.1.seen_ref = f32[8,192,128]{2,1,0:T(8,128)S(1)} collective-permute-done((f32[8,192,128]{2,1,0:T(8,128)S(1)}, f32[8,192,128]{2,1,0:T(8,128)S(1)}, u32[]{:S(2)}, u32[]{:S(2)}) %collective-permute-start.1) | collective-permute-done | bytes 786464 | tf_op jit(solution)/shard_map/ppermute | solution.py:19
  39.6 25.1 %all-gather.5.cloned.1.call-done = f32[1664,512]{1,0:T(8,128)} async-done(((f32[208,512]{1,0:T(8,128)}), f32[1664,512]{1,0:T(8,128)}) %all-gather.5.cloned.1.call-update) | async-done | bytes 3407888 | tf_op jit(solution)/shard_map/all_gather | solution.py:192
  64.7 4.0 %products.1 = (f32[768,128]{1,0:T(8,128)S(1)}, f32[768,128]{1,0:T(8,128)S(1)}) custom-call(s32[2]{0:T(128)S(1)} %pad_add_fusion.place_ref, f32[8,208,512]{2,1,0:T(8,128)} %bitcast.21, f32[8,2,192,128]{3,2,1,0:T(8,128)S(1)} %bitcast.20, f32[8,192,128]{2,1,0:T(8,128)S(1)} %collective-permute-done.1.seen_ref), custom_call_target="tpu_custom_call" | custom-call | tf_op jit(solution)/shard_map/products/pallas_call | solution.py:100
  68.7 0.0 copy-done.1
  68.7 2.6 %collective-permute-start.2 = (f32[768,128]{1,0:T(8,128)S(1)}, f32[768,128]{1,0:T(8,128)S(1)}, u32[]{:S(2)}, u32[]{:S(2)}) collective-permute-start(f32[768,128]{1,0:T(8,128)S(1)} %get-tuple-element.8), channel_id=1, source_target_pairs={{0,16},{16,0},{1,17},{17,1},{2,18},{18,2},{3,19},{19,3},{4,20},{20... | collective-permute-start | bytes 1179656 | tf_op jit(solution)/shard_map/ppermute | solution.py:19
  71.3 1.3 %collective-permute-done.2 = f32[768,128]{1,0:T(8,128)S(1)} collective-permute-done((f32[768,128]{1,0:T(8,128)S(1)}, f32[768,128]{1,0:T(8,128)S(1)}, u32[]{:S(2)}, u32[]{:S(2)}) %collective-permute-start.2) | collective-permute-done | bytes 393248 | tf_op jit(solution)/shard_map/ppermute | solution.py:19
  72.8 0.1 pad_maximum_fusion
  72.8 25.8 %all_to_all.10 = f32[32,32,128]{2,1,0:T(8,128)S(1)} all-to-all(f32[32,32,128]{2,1,0:T(8,128)S(1)} %bitcast.26), channel_id=1, replica_groups=mesh['xl'=2,'z'=8,'core'=2,'y'=8,'xh'=2] {'xl','z','xh'}, dimensions={0} | all-to-all | bytes 1048576 | tf_op jit(solution)/shard_map/all_to_all | solution.py:203
  98.7 12.7 %all_to_all.11 = f32[16,32,128]{2,1,0:T(8,128)S(1)} all-to-all(f32[16,32,128]{2,1,0:T(8,128)S(1)} %broadcast_in_dim.15), channel_id=1, replica_groups=mesh['xl'=2,'z'=8,'core'=2,'y'=8,'xh'=2] {'xl','z'}, dimensions={0} | all-to-all | bytes 524288 | tf_op jit(solution)/shard_map/all_to_all | solution.py:205
  111.4 5.3 %all_gather.19.sums_ref = f32[2,512,128]{2,1,0:T(8,128)} all-gather(f32[1,512,128]{2,1,0:T(8,128)S(1)} %bitcast.27), channel_id=1, replica_groups=mesh['xl'=2,'z'=8,'core'=2,'y'=8,'xh'=2] {'core'}, dimensions={0}, use_global_device_ids=true | all-gather | bytes 786432 | tf_op jit(solution)/shard_map/all_gather | solution.py:207
  116.7 0.0 all-gather.7.cloned.1.call-done
  116.7 6.1 %update.1 = f32[8,2,192,128]{3,2,1,0:T(8,128)} custom-call(s32[2]{0:T(128)} %copy-done.1, f32[8,208,512]{2,1,0:T(8,128)} %bitcast.22, f32[8,208,512]{2,1,0:T(8,128)} %bitcast.24, f32[2,512,128]{2,1,0:T(8,128)} %all_gather.19.sums_ref, f32[8,208,512]{2,1,0:T(8,128)} %bitcast.23, f32[8,208,512]{2,1,0:T(8,128)} %bitcast.25, f32[8,2,192,128]{3,2,1,0:T(8,128)} %bitcast.18), custom_call_target="tpu_custom_call" | custom-call | tf_op jit(solution)/shard_map/update/pallas_call | solution.py:164
  (8 shorter events, 0.2 us)
Async XLA Ops:
  6.5 14.6 %copy-start = (f32[3072,128]{1,0:T(8,128)S(1)}, f32[3072,128]{1,0:T(8,128)}, u32[]{:S(2)}) copy-start(f32[3072,128]{1,0:T(8,128)} %param.5) | copy-start | bytes 4718596
  6.5 58.2 %all-gather.5.cloned.1.call-start = ((), (), s32[]{:S(2)}) async-start(), calls=%async_computation.2 | async-start | bytes 3833856 | tf_op jit(solution)/shard_map/all_gather | solution.py:192
  8.5 108.2 %all-gather.7.cloned.1.call-start = ((), (), s32[]{:S(2)}) async-start(), calls=%async_computation.3 | async-start | bytes 3833856 | tf_op jit(solution)/shard_map/all_gather | solution.py:196
  8.5 11.9 %collective-permute-start = (f32[208,512]{1,0:T(8,128)}, f32[208,512]{1,0:T(8,128)S(1)}, u32[]{:S(2)}, u32[]{:S(2)}) collective-permute-start(f32[208,512]{1,0:T(8,128)} %pack.1), channel_id=1, source_target_pairs={{0,1},{1,0},{2,3},{3,2},{4,5},{5,4},{6,7},{7,6},{8,9},{9,8},{10,11... | collective-permute-start | bytes 1277960 | tf_op jit(solution)/shard_map/ppermute | solution.py:19
  20.4 0.7 copy-start.2
  21.2 18.4 %collective-permute-start.1 = (f32[8,192,128]{2,1,0:T(8,128)S(1)}, f32[8,192,128]{2,1,0:T(8,128)S(1)}, u32[]{:S(2)}, u32[]{:S(2)}) collective-permute-start(f32[8,192,128]{2,1,0:T(8,128)S(1)} %dynamic-slice_bitcast_fusion), channel_id=1, source_target_pairs={{0,1},{1,0},{2,3},{3,2},{4,5},{5,4},{6,7},{7,6},{8,9},{9,8},{10,11... | collective-permute-start | bytes 2359304 | tf_op jit(solution)/shard_map/ppermute | solution.py:19
  26.8 41.9 %copy-start.1 = (s32[2]{0:T(128)}, s32[2]{0:T(128)S(1)}, u32[]{:S(2)}) copy-start(s32[2]{0:T(128)S(1)} %pad_add_fusion.place_ref) | copy-start | bytes 28
  68.7 3.9 %collective-permute-start.2 = (f32[768,128]{1,0:T(8,128)S(1)}, f32[768,128]{1,0:T(8,128)S(1)}, u32[]{:S(2)}, u32[]{:S(2)}) collective-permute-start(f32[768,128]{1,0:T(8,128)S(1)} %get-tuple-element.8), channel_id=1, source_target_pairs={{0,16},{16,0},{1,17},{17,1},{2,18},{18,2},{3,19},{19,3},{4,20},{20... | collective-permute-start | bytes 1179656 | tf_op jit(solution)/shard_map/ppermute | solution.py:19
Sparse Core Ops, SparseCore 0:
  9.4 55.2 all-gather.4
  66.8 48.7 all-gather.6

commit v4 on v3

--- a/solution.py
+++ b/solution.py
@@ -19,29 +19,29 @@
     return lax.ppermute(value, axis, [(0, 1), (1, 0)])
 
 
+def together(*values):
+    return lax.optimization_barrier(values)
+
+
 def split(value):
     high = value.astype(jnp.bfloat16)
     return high, (value - high.astype(jnp.float32)).astype(jnp.bfloat16)
 
 
-def pack_kernel(one_ref, two_ref, tri_one_ref, tri_two_ref, out_ref):
-    out_ref[:ROWS, :256] = one_ref[...]
-    out_ref[:ROWS, 256:] = two_ref[...]
-    for i, ref in enumerate((tri_one_ref, tri_two_ref)):
-        at = pl.ds(ROWS + 8 * i, 8)
-        out_ref[at, :256] = ref[:8]
-        out_ref[at, 256:] = ref[8:]
-
-
-def pack(panel_one, panel_two, factor_one, factor_two):
+def pack_kernel(one_ref, two_ref, out_ref):
+    out_ref[:, :256] = one_ref[...]
+    out_ref[:, 256:] = two_ref[...]
+
+
+def pack(panel_one, panel_two):
     vmem = pl.BlockSpec(memory_space=pltpu.VMEM)
     return pl.pallas_call(
         pack_kernel,
-        out_shape=jax.ShapeDtypeStruct((ROWS + 16, 512), jnp.float32),
-        in_specs=[vmem] * 4,
+        out_shape=jax.ShapeDtypeStruct((ROWS, 512), jnp.float32),
+        in_specs=[vmem] * 2,
         out_specs=vmem,
         name="pack",
-    )(panel_one, panel_two, factor_one, factor_two)
+    )(panel_one, panel_two)
 
 
 def products_kernel(
@@ -50,7 +50,7 @@
     side, core = place_ref[0], place_ref[1]
     step = pl.program_id(0)
     count = near_ref.shape[0]
-    left = near_ref[:, :ROWS, :].reshape(count * ROWS, 512)
+    left = near_ref[...].reshape(count * ROWS, 512)
     right = jnp.concatenate(
         [
             mine_ref[:, side].reshape(count * ROWS, 128),
@@ -103,7 +103,7 @@
         out_shape=[jax.ShapeDtypeStruct((768, 128), jnp.float32)] * 2,
         in_specs=[
             pl.BlockSpec(memory_space=pltpu.SMEM),
-            pl.BlockSpec((count, ROWS + 16, 512), lambda i: (i, 0, 0)),
+            pl.BlockSpec((count, ROWS, 512), lambda i: (i, 0, 0)),
             pl.BlockSpec((count, 2, ROWS, 128), lambda i: (i, 0, 0, 0)),
             pl.BlockSpec((count, ROWS, 128), lambda i: (i, 0, 0)),
         ],
@@ -126,8 +126,7 @@
 
 
 def update_kernel(
-    place_ref, near_ref, far_ref, sums_ref, near_tri_ref, far_tri_ref, old_ref,
-    out_ref, coeffs, tri,
+    place_ref, near_ref, far_ref, sums_ref, tri_ref, old_ref, out_ref, coeffs
 ):
     side = place_ref[0]
     count = near_ref.shape[0]
@@ -140,26 +139,19 @@
                 for h in range(2)
             ]
         )
-        for ref, which in ((near_tri_ref, side), (far_tri_ref, 1 - side)):
-            for i in range(2):
-                for j in range(2):
-                    tri[i, :, which, pl.ds(8 * j, 8), :] = ref[
-                        :, pl.ds(8 * i, 8), pl.ds(256 * j, 256)
-                    ]
-        tri_one, tri_two = (split(tri[i].reshape(256, 256)) for i in range(2))
-        coeff_two = triple(tri_two, split(sums_ref[1, :256]))
+        coeff_two = triple(split(tri_ref[1]), split(sums_ref[1, :256]))
         moved = sums_ref[0, :256] - triple(split(cross), split(coeff_two))
-        coeffs[:256] = triple(tri_one, split(moved))
+        coeffs[:256] = triple(split(tri_ref[0]), split(moved))
         coeffs[256:] = coeff_two
 
     right = split(coeffs[...])
     for ref, which in ((near_ref, side), (far_ref, 1 - side)):
-        panel = ref[:, :ROWS, :].reshape(count * ROWS, 512)
+        panel = ref[...].reshape(count * ROWS, 512)
         change = triple(split(panel), right).reshape(count, ROWS, 128)
         out_ref[:, which] = old_ref[:, which] - change
 
 
-def update(place, near, far, sums, by_owner):
+def update(place, near, far, sums, tri, by_owner):
     count = 4
     return pl.pallas_call(
         update_kernel,
@@ -167,33 +159,40 @@
         out_shape=jax.ShapeDtypeStruct(by_owner.shape, jnp.float32),
         in_specs=[
             pl.BlockSpec(memory_space=pltpu.SMEM),
-            pl.BlockSpec((count, ROWS + 16, 512), lambda i: (i, 0, 0)),
-            pl.BlockSpec((count, ROWS + 16, 512), lambda i: (i, 0, 0)),
+            pl.BlockSpec((count, ROWS, 512), lambda i: (i, 0, 0)),
+            pl.BlockSpec((count, ROWS, 512), lambda i: (i, 0, 0)),
             pl.BlockSpec((2, 512, 128), lambda i: (0, 0, 0)),
-            pl.BlockSpec((NY, 16, 512), lambda i: (0, ROWS // 16, 0)),
-            pl.BlockSpec((NY, 16, 512), lambda i: (0, ROWS // 16, 0)),
+            pl.BlockSpec((2, 256, 256), lambda i: (0, 0, 0)),
             pl.BlockSpec((count, 2, ROWS, 128), lambda i: (i, 0, 0, 0)),
         ],
         out_specs=pl.BlockSpec((count, 2, ROWS, 128), lambda i: (i, 0, 0, 0)),
-        scratch_shapes=[
-            pltpu.VMEM((512, 128), jnp.float32),
-            pltpu.VMEM((2, NY, 2, 16, 256), jnp.float32),
-        ],
+        scratch_shapes=[pltpu.VMEM((512, 128), jnp.float32)],
         compiler_params=pltpu.CompilerParams(vmem_limit_bytes=60 * MIB),
         name="update",
-    )(place, near, far, sums, near, far, by_owner)
+    )(place, near, far, sums, tri, by_owner)
 
 
 def shards(vectors, panel_one, factor_one, panel_two, factor_two):
     side, core = lax.axis_index("xh"), lax.axis_index("core")
     place = jnp.stack([side, core]).astype(jnp.int32)
 
-    own = pack(panel_one, panel_two, factor_one, factor_two)
+    own = pack(panel_one, panel_two)
     near = lax.all_gather(own, "y", axis=0)
     by_owner = vectors.reshape(NY, 2, ROWS, 128)
     theirs = lax.dynamic_index_in_dim(by_owner, 1 - side, 1, False)
     seen = swap(theirs, "xh")
-    far = lax.all_gather(swap(own, "xh"), "y", axis=0)
+
+    tri = jnp.where(core == 0, factor_one, factor_two).reshape(8, 4, 128)
+    tri = lax.dynamic_index_in_dim(tri, lax.axis_index("z"), 0, False)
+    tri, _ = together(jnp.broadcast_to(tri[None], (16, 4, 128)), own)
+    tri = lax.all_to_all(tri, ("y", "xh"), 0, 0).reshape(64, 128)
+    far, tri = together(swap(own, "xh"), tri)
+    far = lax.all_gather(far, "y", axis=0)
+    tri = jnp.broadcast_to(tri[None], (8, 64, 128))
+    tri = lax.all_to_all(tri, "z", 0, 0).reshape(8, 16, 2, 256)
+    tri = tri.transpose(1, 0, 2, 3).reshape(256, 256)
+    tri = lax.all_gather(tri, "core", axis=0)
+    near, tri = together(near, tri)
 
     keep, send = products(place, near, by_owner, seen)
     part = keep + swap(send, "core")
@@ -205,7 +204,7 @@
     part = lax.all_to_all(spread, ("xl", "z"), 0, 0)
     part = part.reshape(16, 2, 16, 128).transpose(1, 0, 2, 3).reshape(512, 128)
     sums = lax.all_gather(part, "core", axis=0)
-    return update(place, near, far, sums, by_owner).reshape(vectors.shape)
+    return update(place, near, far, sums, tri, by_owner).reshape(vectors.shape)
 
 
 def solution(mesh):

time: 130 us -> 128 us (0.985)
  waiting for transfers between devices: 45.6 us -> 11.1 us
  blocking collectives: 43.7 us -> 65.8 us
  starting transfers between devices: 13.6 us -> 21 us
  local copies, waits for them, and re-layouts: 0.91 us -> 2.95 us
    all_gather x1, waiting for transfers between devices: 25.1 us -> 0.34 us  [shards(): near = lax.all_gather(own, 'y', axis=0)]
    ppermute x3, waiting for transfers between devices: 20.5 us -> 1.33 us  [swap(): return lax.ppermute(value, axis, [(0, 1), (1, 0)])]
    all_to_all x0 -> x1, blocking collectives: none -> 15.9 us  [shards(): tri = lax.all_to_all(tri, ('y', 'xh'), 0, 0).reshape(64, 128)]
    all_to_all x0 -> x1, starting transfers between devices: none -> 10.1 us  [shards(): tri = lax.all_to_all(tri, 'z', 0, 0).reshape(8, 16, 2, 256)]
    all_to_all x0 -> x1, waiting for transfers between devices: none -> 9.36 us  [shards(): tri = lax.all_to_all(tri, 'z', 0, 0).reshape(8, 16, 2, 256)]
    all_gather x0 -> x1, blocking collectives: none -> 6.19 us  [shards(): tri = lax.all_gather(tri, 'core', axis=0)]
    ppermute x3, starting transfers between devices: 13.6 us -> 10.9 us  [swap(): return lax.ppermute(value, axis, [(0, 1), (1, 0)])]
  transfers between devices with their start and end apart: 5 -> 6, of which waited for: 4 -> 3; matrix products, arithmetic and copies ran while one was open for 0% -> 2% of each run, Pallas kernels for 3% -> 3%
where the time goes in v4:
time: 128 us
  blocking collectives  65.8 us (51%)
  starting transfers between devices  21 us (16%)
  between operations  13.6 us (11%)
  Pallas kernels  12.3 us (10%)
  waiting for transfers between devices  11.1 us (9%)
  local copies, waits for them, and re-layouts  2.95 us (2%)
    all_to_all x1, blocking collectives, shards(): parts = lax.all_to_all(parts, ('xl', 'z', 'xh'), 0, 0)  25.8 us
    all_to_all x1, blocking collectives, shards(): tri = lax.all_to_all(tri, ('y', 'xh'), 0, 0).reshape(64, 128)  15.9 us
    all_to_all x1, blocking collectives, shards(): part = lax.all_to_all(spread, ('xl', 'z'), 0, 0)  12.7 us
    ppermute x3, starting transfers between devices, swap(): return lax.ppermute(value, axis, [(0, 1), (1, 0)])  10.9 us
    all_to_all x1, starting transfers between devices, shards(): tri = lax.all_to_all(tri, 'z', 0, 0).reshape(8, 16, 2, 256)  10.1 us
    all_to_all x1, waiting for transfers between devices, shards(): tri = lax.all_to_all(tri, 'z', 0, 0).reshape(8, 16, 2, 256)  9.36 us
    pallas_call x1, Pallas kernels, update(): pl.pallas_call(update_kernel, grid=(NY // count,), out_shape=jax.ShapeDty...  6.44 us
    all_gather x1, blocking collectives, shards(): tri = lax.all_gather(tri, 'core', axis=0)  6.19 us
  transfers between devices with their start and end apart: 6, of which 3 were waited for; matrix products, arithmetic and copies ran while one was open for 2% of the time, Pallas kernels for 3%

profile of v4, /device:TPU:1, one launch (start us, length us, event | category | flops | bytes accessed | tf_op | source)
XLA Modules:
  0.0 127.6 jit_solution(12913767291042974627)
XLA Ops:
  6.5 0.0 copy-start
  6.5 0.0 all-gather.5.cloned.1.call-start
  6.5 1.9 %pack.1 = f32[192,512]{1,0:T(8,128)} custom-call(f32[192,256]{1,0:T(8,128)} %one_ref.1, f32[192,256]{1,0:T(8,128)} %two_ref.1), custom_call_target="tpu_custom_call" | custom-call | tf_op jit(solution)/shard_map/pack/pallas_call | solution.py:38
  8.5 0.0 all-gather.5.cloned.1.call-update
  8.5 0.0 all-gather.7.cloned.1.call-start
  8.5 5.5 %collective-permute-start = (f32[192,512]{1,0:T(8,128)}, f32[192,512]{1,0:T(8,128)S(1)}, u32[]{:S(2)}, u32[]{:S(2)}) collective-permute-start(f32[192,512]{1,0:T(8,128)} %pack.1), channel_id=1, source_target_pairs={{0,1},{1,0},{2,3},{3,2},{4,5},{5,4},{6,7},{7,6},{8,9},{9,8},{10,11... | collective-permute-start | bytes 1179656 | tf_op jit(solution)/shard_map/ppermute | solution.py:19
  14.0 0.7 broadcast_select_fusion
  14.8 15.9 %all_to_all.20 = f32[16,4,128]{2,1,0:T(4,128)S(1)} all-to-all(f32[16,4,128]{2,1,0:T(4,128)S(1)} %broadcast_in_dim.13), channel_id=1, replica_groups=mesh['xl'=2,'z'=8,'core'=2,'y'=8,'xh'=2] {'y','xh'}, dimensions={0} | all-to-all | bytes 65536 | tf_op jit(solution)/shard_map/all_to_all | solution.py:188
  30.7 0.0 collective-permute-done
  30.7 0.0 copy-start.2
  30.7 0.7 copy-done.2
  31.4 0.0 all-gather.7.cloned.1.call-update
  31.4 0.0 copy-done
  31.5 0.9 dynamic-slice_bitcast_fusion
  32.4 2.2 %collective-permute-start.1 = (f32[8,192,128]{2,1,0:T(8,128)}, f32[8,192,128]{2,1,0:T(8,128)S(1)}, u32[]{:S(2)}, u32[]{:S(2)}) collective-permute-start(f32[8,192,128]{2,1,0:T(8,128)} %dynamic-slice_bitcast_fusion), channel_id=1, source_target_pairs={{0,1},{1,0},{2,3},{3,2},{4,5},{5,4},{6,7},{7,6},{8,9},{9,8},{10,11... | collective-permute-start | bytes 2359304 | tf_op jit(solution)/shard_map/ppermute | solution.py:19
  34.6 0.7 broadcast_in_dim.14
  35.4 10.1 %all-to-all-start.1 = ((f32[8,64,128]{2,1,0:T(8,128)}), f32[8,64,128]{2,1,0:T(8,128)S(1)}, u32[]{:S(2)}, u32[]{:S(2)}) async-start(f32[8,64,128]{2,1,0:T(8,128)} %broadcast_in_dim.14), calls=%async_computation.1 | async-start | bytes 524288 | tf_op jit(solution)/shard_map/all_to_all | solution.py:192
  45.4 0.1 pad_add_fusion.place_ref
  45.5 0.0 copy-start.1
  45.5 9.4 %all-to-all-done.1 = f32[8,64,128]{2,1,0:T(8,128)S(1)} async-done(((f32[8,64,128]{2,1,0:T(8,128)}), f32[8,64,128]{2,1,0:T(8,128)S(1)}, u32[]{:S(2)}, u32[]{:S(2)}) %all-to-all-start.1) | async-done | bytes 262176 | tf_op jit(solution)/shard_map/all_to_all | solution.py:192
  54.9 0.2 reshape.30
  55.0 0.1 copy.10
  55.1 0.2 all_gather_reshape.6
  55.3 6.2 %all_gather.20.tri_ref = f32[2,256,256]{2,1,0:T(8,128)} all-gather(f32[1,256,256]{2,1,0:T(8,128)S(1)} %all_gather_reshape.6), channel_id=1, replica_groups=mesh['xl'=2,'z'=8,'core'=2,'y'=8,'xh'=2] {'core'}, dimensions={0}, use_global_device_ids=true | all-gather | bytes 786432 | tf_op jit(solution)/shard_map/all_gather | solution.py:194
  61.5 0.3 all-gather.5.cloned.1.call-done
  61.8 0.0 collective-permute-done.1.seen_ref
  61.8 3.9 %products.1 = (f32[768,128]{1,0:T(8,128)S(1)}, f32[768,128]{1,0:T(8,128)S(1)}) custom-call(s32[2]{0:T(128)S(1)} %pad_add_fusion.place_ref, f32[8,192,512]{2,1,0:T(8,128)} %bitcast.25, f32[8,2,192,128]{3,2,1,0:T(8,128)S(1)} %bitcast.24, f32[8,192,128]{2,1,0:T(8,128)S(1)} %collective-permute-done.1.seen_ref), custom_call_target="tpu_custom_call" | custom-call | tf_op jit(solution)/shard_map/products/pallas_call | solution.py:100
  65.8 0.0 copy-done.1
  65.8 3.2 %collective-permute-start.2 = (f32[768,128]{1,0:T(8,128)S(1)}, f32[768,128]{1,0:T(8,128)S(1)}, u32[]{:S(2)}, u32[]{:S(2)}) collective-permute-start(f32[768,128]{1,0:T(8,128)S(1)} %get-tuple-element.17), channel_id=1, source_target_pairs={{0,16},{16,0},{1,17},{17,1},{2,18},{18,2},{3,19},{19,3},{4,20},{20... | collective-permute-start | bytes 1179656 | tf_op jit(solution)/shard_map/ppermute | solution.py:19
  69.0 1.3 %collective-permute-done.2 = f32[768,128]{1,0:T(8,128)S(1)} collective-permute-done((f32[768,128]{1,0:T(8,128)S(1)}, f32[768,128]{1,0:T(8,128)S(1)}, u32[]{:S(2)}, u32[]{:S(2)}) %collective-permute-start.2) | collective-permute-done | bytes 393248 | tf_op jit(solution)/shard_map/ppermute | solution.py:19
  70.4 0.1 pad_maximum_fusion
  70.5 25.8 %all_to_all.21 = f32[32,32,128]{2,1,0:T(8,128)S(1)} all-to-all(f32[32,32,128]{2,1,0:T(8,128)S(1)} %bitcast.28), channel_id=1, replica_groups=mesh['xl'=2,'z'=8,'core'=2,'y'=8,'xh'=2] {'xl','z','xh'}, dimensions={0} | all-to-all | bytes 1048576 | tf_op jit(solution)/shard_map/all_to_all | solution.py:202
  96.4 12.7 %all_to_all.22 = f32[16,32,128]{2,1,0:T(8,128)S(1)} all-to-all(f32[16,32,128]{2,1,0:T(8,128)S(1)} %broadcast_in_dim.32), channel_id=1, replica_groups=mesh['xl'=2,'z'=8,'core'=2,'y'=8,'xh'=2] {'xl','z'}, dimensions={0} | all-to-all | bytes 524288 | tf_op jit(solution)/shard_map/all_to_all | solution.py:204
  109.1 5.3 %all_gather.23.sums_ref = f32[2,512,128]{2,1,0:T(8,128)} all-gather(f32[1,512,128]{2,1,0:T(8,128)S(1)} %bitcast.29), channel_id=1, replica_groups=mesh['xl'=2,'z'=8,'core'=2,'y'=8,'xh'=2] {'core'}, dimensions={0}, use_global_device_ids=true | all-gather | bytes 786432 | tf_op jit(solution)/shard_map/all_gather | solution.py:206
  114.3 0.0 all-gather.7.cloned.1.call-done
  114.3 6.4 %update.1 = f32[8,2,192,128]{3,2,1,0:T(8,128)} custom-call(s32[2]{0:T(128)} %copy-done.1, f32[8,192,512]{2,1,0:T(8,128)} %bitcast.26, f32[8,192,512]{2,1,0:T(8,128)} %bitcast.27, f32[2,512,128]{2,1,0:T(8,128)} %all_gather.23.sums_ref, f32[2,256,256]{2,1,0:T(8,128)} %all_gather.20.tri_ref, f32[8,2,192,128]{3,2,1,0:T(8,128)} %bitcast.22), custom_call_target="tpu_custom_call" | custom-call | tf_op jit(solution)/shard_map/update/pallas_call | solution.py:156
  (11 shorter events, 0.2 us)
Async XLA Ops:
  6.5 24.9 %copy-start = (f32[3072,128]{1,0:T(8,128)S(1)}, f32[3072,128]{1,0:T(8,128)}, u32[]{:S(2)}) copy-start(f32[3072,128]{1,0:T(8,128)} %param.5) | copy-start | bytes 4718596
  6.5 55.3 %all-gather.5.cloned.1.call-start = ((), (), s32[]{:S(2)}) async-start(), calls=%async_computation.4 | async-start | bytes 3538944 | tf_op jit(solution)/shard_map/all_gather | solution.py:180
  8.5 105.8 %all-gather.7.cloned.1.call-start = ((), (), s32[]{:S(2)}) async-start(), calls=%async_computation.5 | async-start | bytes 3538944 | tf_op jit(solution)/shard_map/all_gather | solution.py:190
  8.5 22.1 %collective-permute-start = (f32[192,512]{1,0:T(8,128)}, f32[192,512]{1,0:T(8,128)S(1)}, u32[]{:S(2)}, u32[]{:S(2)}) collective-permute-start(f32[192,512]{1,0:T(8,128)} %pack.1), channel_id=1, source_target_pairs={{0,1},{1,0},{2,3},{3,2},{4,5},{5,4},{6,7},{7,6},{8,9},{9,8},{10,11... | collective-permute-start | bytes 1179656 | tf_op jit(solution)/shard_map/ppermute | solution.py:19
  30.7 0.7 copy-start.2
  32.4 29.4 %collective-permute-start.1 = (f32[8,192,128]{2,1,0:T(8,128)}, f32[8,192,128]{2,1,0:T(8,128)S(1)}, u32[]{:S(2)}, u32[]{:S(2)}) collective-permute-start(f32[8,192,128]{2,1,0:T(8,128)} %dynamic-slice_bitcast_fusion), channel_id=1, source_target_pairs={{0,1},{1,0},{2,3},{3,2},{4,5},{5,4},{6,7},{7,6},{8,9},{9,8},{10,11... | collective-permute-start | bytes 2359304 | tf_op jit(solution)/shard_map/ppermute | solution.py:19
  35.4 19.5 %all-to-all-start.1 = ((f32[8,64,128]{2,1,0:T(8,128)}), f32[8,64,128]{2,1,0:T(8,128)S(1)}, u32[]{:S(2)}, u32[]{:S(2)}) async-start(f32[8,64,128]{2,1,0:T(8,128)} %broadcast_in_dim.14), calls=%async_computation.1 | async-start | bytes 524288 | tf_op jit(solution)/shard_map/all_to_all | solution.py:192
  45.5 20.3 %copy-start.1 = (s32[2]{0:T(128)}, s32[2]{0:T(128)S(1)}, u32[]{:S(2)}) copy-start(s32[2]{0:T(128)S(1)} %pad_add_fusion.place_ref) | copy-start | bytes 28
  65.8 4.5 %collective-permute-start.2 = (f32[768,128]{1,0:T(8,128)S(1)}, f32[768,128]{1,0:T(8,128)S(1)}, u32[]{:S(2)}, u32[]{:S(2)}) collective-permute-start(f32[768,128]{1,0:T(8,128)S(1)} %get-tuple-element.17), channel_id=1, source_target_pairs={{0,16},{16,0},{1,17},{17,1},{2,18},{18,2},{3,19},{19,3},{4,20},{20... | collective-permute-start | bytes 1179656 | tf_op jit(solution)/shard_map/ppermute | solution.py:19
Sparse Core Ops, SparseCore 0:
  9.4 52.3 all-gather.4
  63.9 46.4 all-gather.6

commit v5 on v4

--- a/solution.py
+++ b/solution.py
@@ -195,7 +195,8 @@
     near, tri = together(near, tri)
 
     keep, send = products(place, near, by_owner, seen)
-    part = keep + swap(send, "core")
+    sent = lax.all_gather(send, "core", axis=0)
+    part = keep + lax.dynamic_index_in_dim(sent, 1 - core, 0, False)
     inner = part[:512].reshape(2, 16, 16, 128).transpose(1, 0, 2, 3)
     cross = jnp.broadcast_to(part[512:].reshape(16, 1, 16, 128), (16, 2, 16, 128))
     parts = jnp.concatenate([inner, cross], axis=2).reshape(32, 32, 128)

time: 128 us -> 127 us (level)
  blocking collectives: 65.8 us -> 69 us
  starting transfers between devices: 21 us -> 17.8 us
  waiting for transfers between devices: 11.1 us -> 9.72 us
    all_gather x0 -> x1, blocking collectives: none -> 3.31 us  [shards(): sent = lax.all_gather(send, 'core', axis=0)]
    ppermute x3 -> x2, starting transfers between devices: 10.9 us -> 7.72 us  [swap(): return lax.ppermute(value, axis, [(0, 1), (1, 0)])]
    ppermute x3 -> x2, waiting for transfers between devices: 1.33 us -> 0.01 us  [swap(): return lax.ppermute(value, axis, [(0, 1), (1, 0)])]
  transfers between devices with their start and end apart: 6 -> 5, of which waited for: 3 -> 2; matrix products, arithmetic and copies ran while one was open for 2% -> 2% of each run, Pallas kernels for 3% -> 3%
where the time goes in v5:
time: 127 us; the launch traced here: 126 us
  blocking collectives  69 us (54%)
  starting transfers between devices  17.8 us (14%)
  between operations  13.6 us (11%)
  Pallas kernels  12.3 us (10%)
  waiting for transfers between devices  9.72 us (8%)
  local copies, waits for them, and re-layouts  2.95 us (2%)
    all_to_all x1, blocking collectives, shards(): parts = lax.all_to_all(parts, ('xl', 'z', 'xh'), 0, 0)  25.8 us
    all_to_all x1, blocking collectives, shards(): tri = lax.all_to_all(tri, ('y', 'xh'), 0, 0).reshape(64, 128)  15.9 us
    all_to_all x1, blocking collectives, shards(): part = lax.all_to_all(spread, ('xl', 'z'), 0, 0)  12.7 us
    all_to_all x1, starting transfers between devices, shards(): tri = lax.all_to_all(tri, 'z', 0, 0).reshape(8, 16, 2, 256)  10.1 us
    all_to_all x1, waiting for transfers between devices, shards(): tri = lax.all_to_all(tri, 'z', 0, 0).reshape(8, 16, 2, 256)  9.36 us
    ppermute x2, starting transfers between devices, swap(): return lax.ppermute(value, axis, [(0, 1), (1, 0)])  7.72 us
    pallas_call x1, Pallas kernels, update(): pl.pallas_call(update_kernel, grid=(NY // count,), out_shape=jax.ShapeDty...  6.44 us
    all_gather x1, blocking collectives, shards(): tri = lax.all_gather(tri, 'core', axis=0)  6.18 us
  transfers between devices with their start and end apart: 5, of which 2 were waited for; matrix products, arithmetic and copies ran while one was open for 2% of the time, Pallas kernels for 3%

profile of v5, /device:TPU:1, one launch (start us, length us, event | category | flops | bytes accessed | tf_op | source)
XLA Modules:
  0.0 126.4 jit_solution(12022325214666080970)
XLA Ops:
  6.5 0.0 copy-start
  6.5 0.0 all-gather.6.cloned.1.call-start
  6.5 1.9 %pack.1 = f32[192,512]{1,0:T(8,128)} custom-call(f32[192,256]{1,0:T(8,128)} %one_ref.1, f32[192,256]{1,0:T(8,128)} %two_ref.1), custom_call_target="tpu_custom_call" | custom-call | tf_op jit(solution)/shard_map/pack/pallas_call | solution.py:38
  8.5 0.0 all-gather.6.cloned.1.call-update
  8.5 0.0 all-gather.8.cloned.1.call-start
  8.6 5.5 %collective-permute-start = (f32[192,512]{1,0:T(8,128)}, f32[192,512]{1,0:T(8,128)S(1)}, u32[]{:S(2)}, u32[]{:S(2)}) collective-permute-start(f32[192,512]{1,0:T(8,128)} %pack.1), channel_id=1, source_target_pairs={{0,1},{1,0},{2,3},{3,2},{4,5},{5,4},{6,7},{7,6},{8,9},{9,8},{10,11... | collective-permute-start | bytes 1179656 | tf_op jit(solution)/shard_map/ppermute | solution.py:19
  14.1 0.7 broadcast_select_fusion
  14.8 15.9 %all_to_all.20 = f32[16,4,128]{2,1,0:T(4,128)S(1)} all-to-all(f32[16,4,128]{2,1,0:T(4,128)S(1)} %broadcast_in_dim.13), channel_id=1, replica_groups=mesh['xl'=2,'z'=8,'core'=2,'y'=8,'xh'=2] {'y','xh'}, dimensions={0} | all-to-all | bytes 65536 | tf_op jit(solution)/shard_map/all_to_all | solution.py:188
  30.7 0.0 collective-permute-done
  30.7 0.0 copy-start.2
  30.7 0.7 copy-done.2
  31.4 0.0 all-gather.8.cloned.1.call-update
  31.5 0.0 copy-done
  31.5 0.9 dynamic-slice_bitcast_fusion
  32.4 2.2 %collective-permute-start.1 = (f32[8,192,128]{2,1,0:T(8,128)}, f32[8,192,128]{2,1,0:T(8,128)S(1)}, u32[]{:S(2)}, u32[]{:S(2)}) collective-permute-start(f32[8,192,128]{2,1,0:T(8,128)} %dynamic-slice_bitcast_fusion), channel_id=1, source_target_pairs={{0,1},{1,0},{2,3},{3,2},{4,5},{5,4},{6,7},{7,6},{8,9},{9,8},{10,11... | collective-permute-start | bytes 2359304 | tf_op jit(solution)/shard_map/ppermute | solution.py:19
  34.7 0.7 broadcast_in_dim.14
  35.4 10.1 %all-to-all-start.1 = ((f32[8,64,128]{2,1,0:T(8,128)}), f32[8,64,128]{2,1,0:T(8,128)S(1)}, u32[]{:S(2)}, u32[]{:S(2)}) async-start(f32[8,64,128]{2,1,0:T(8,128)} %broadcast_in_dim.14), calls=%async_computation.1 | async-start | bytes 524288 | tf_op jit(solution)/shard_map/all_to_all | solution.py:192
  45.4 0.1 pad_add_fusion.place_ref
  45.5 0.0 copy-start.1
  45.5 9.4 %all-to-all-done.1 = f32[8,64,128]{2,1,0:T(8,128)S(1)} async-done(((f32[8,64,128]{2,1,0:T(8,128)}), f32[8,64,128]{2,1,0:T(8,128)S(1)}, u32[]{:S(2)}, u32[]{:S(2)}) %all-to-all-start.1) | async-done | bytes 262176 | tf_op jit(solution)/shard_map/all_to_all | solution.py:192
  54.9 0.2 reshape.30
  55.0 0.1 copy.10
  55.1 0.2 all_gather_reshape.6
  55.3 6.2 %all_gather.26.tri_ref = f32[2,256,256]{2,1,0:T(8,128)} all-gather(f32[1,256,256]{2,1,0:T(8,128)S(1)} %all_gather_reshape.6), channel_id=1, replica_groups=mesh['xl'=2,'z'=8,'core'=2,'y'=8,'xh'=2] {'core'}, dimensions={0}, use_global_device_ids=true | all-gather | bytes 786432 | tf_op jit(solution)/shard_map/all_gather | solution.py:194
  61.5 0.3 all-gather.6.cloned.1.call-done
  61.8 0.0 collective-permute-done.1.seen_ref
  61.8 3.9 %products.1 = (f32[768,128]{1,0:T(8,128)S(1)}, f32[768,128]{1,0:T(8,128)S(1)}) custom-call(s32[2]{0:T(128)S(1)} %pad_add_fusion.place_ref, f32[8,192,512]{2,1,0:T(8,128)} %bitcast.28, f32[8,2,192,128]{3,2,1,0:T(8,128)S(1)} %bitcast.27, f32[8,192,128]{2,1,0:T(8,128)S(1)} %collective-permute-done.1.seen_ref), custom_call_target="tpu_custom_call" | custom-call | tf_op jit(solution)/shard_map/products/pallas_call | solution.py:100
  65.7 0.0 copy-done.1
  65.8 3.3 %all-gather.2 = f32[1536,128]{1,0:T(8,128)S(1)} all-gather(f32[768,128]{1,0:T(8,128)S(1)} %get-tuple-element.17), channel_id=4, replica_groups=mesh['xl'=2,'z'=8,'core'=2,'y'=8,'xh'=2] {'core'}, dimensions={0}, use_global_device_ids=true | all-gather | bytes 1179648 | tf_op jit(solution)/shard_map/all_gather | solution.py:198
  69.2 0.1 pad_maximum_fusion
  69.3 25.8 %all_to_all.21 = f32[32,32,128]{2,1,0:T(8,128)S(1)} all-to-all(f32[32,32,128]{2,1,0:T(8,128)S(1)} %bitcast.31), channel_id=1, replica_groups=mesh['xl'=2,'z'=8,'core'=2,'y'=8,'xh'=2] {'xl','z','xh'}, dimensions={0} | all-to-all | bytes 1048576 | tf_op jit(solution)/shard_map/all_to_all | solution.py:203
  95.1 12.7 %all_to_all.22 = f32[16,32,128]{2,1,0:T(8,128)S(1)} all-to-all(f32[16,32,128]{2,1,0:T(8,128)S(1)} %broadcast_in_dim.32), channel_id=1, replica_groups=mesh['xl'=2,'z'=8,'core'=2,'y'=8,'xh'=2] {'xl','z'}, dimensions={0} | all-to-all | bytes 524288 | tf_op jit(solution)/shard_map/all_to_all | solution.py:205
  107.8 5.3 %all_gather.31.sums_ref = f32[2,512,128]{2,1,0:T(8,128)} all-gather(f32[1,512,128]{2,1,0:T(8,128)S(1)} %bitcast.33), channel_id=1, replica_groups=mesh['xl'=2,'z'=8,'core'=2,'y'=8,'xh'=2] {'core'}, dimensions={0}, use_global_device_ids=true | all-gather | bytes 786432 | tf_op jit(solution)/shard_map/all_gather | solution.py:207
  113.1 0.0 all-gather.8.cloned.1.call-done
  113.1 6.4 %update.1 = f32[8,2,192,128]{3,2,1,0:T(8,128)} custom-call(s32[2]{0:T(128)} %copy-done.1, f32[8,192,512]{2,1,0:T(8,128)} %bitcast.29, f32[8,192,512]{2,1,0:T(8,128)} %bitcast.30, f32[2,512,128]{2,1,0:T(8,128)} %all_gather.31.sums_ref, f32[2,256,256]{2,1,0:T(8,128)} %all_gather.26.tri_ref, f32[8,2,192,128]{3,2,1,0:T(8,128)} %bitcast.25), custom_call_target="tpu_custom_call" | custom-call | tf_op jit(solution)/shard_map/update/pallas_call | solution.py:156
  (11 shorter events, 0.2 us)
Async XLA Ops:
  6.5 24.9 %copy-start = (f32[3072,128]{1,0:T(8,128)S(1)}, f32[3072,128]{1,0:T(8,128)}, u32[]{:S(2)}) copy-start(f32[3072,128]{1,0:T(8,128)} %param.5) | copy-start | bytes 4718596
  6.5 55.3 %all-gather.6.cloned.1.call-start = ((), (), s32[]{:S(2)}) async-start(), calls=%async_computation.4 | async-start | bytes 3538944 | tf_op jit(solution)/shard_map/all_gather | solution.py:180
  8.5 104.6 %all-gather.8.cloned.1.call-start = ((), (), s32[]{:S(2)}) async-start(), calls=%async_computation.5 | async-start | bytes 3538944 | tf_op jit(solution)/shard_map/all_gather | solution.py:190
  8.6 22.1 %collective-permute-start = (f32[192,512]{1,0:T(8,128)}, f32[192,512]{1,0:T(8,128)S(1)}, u32[]{:S(2)}, u32[]{:S(2)}) collective-permute-start(f32[192,512]{1,0:T(8,128)} %pack.1), channel_id=1, source_target_pairs={{0,1},{1,0},{2,3},{3,2},{4,5},{5,4},{6,7},{7,6},{8,9},{9,8},{10,11... | collective-permute-start | bytes 1179656 | tf_op jit(solution)/shard_map/ppermute | solution.py:19
  30.7 0.7 copy-start.2
  32.4 29.4 %collective-permute-start.1 = (f32[8,192,128]{2,1,0:T(8,128)}, f32[8,192,128]{2,1,0:T(8,128)S(1)}, u32[]{:S(2)}, u32[]{:S(2)}) collective-permute-start(f32[8,192,128]{2,1,0:T(8,128)} %dynamic-slice_bitcast_fusion), channel_id=1, source_target_pairs={{0,1},{1,0},{2,3},{3,2},{4,5},{5,4},{6,7},{7,6},{8,9},{9,8},{10,11... | collective-permute-start | bytes 2359304 | tf_op jit(solution)/shard_map/ppermute | solution.py:19
  35.4 19.5 %all-to-all-start.1 = ((f32[8,64,128]{2,1,0:T(8,128)}), f32[8,64,128]{2,1,0:T(8,128)S(1)}, u32[]{:S(2)}, u32[]{:S(2)}) async-start(f32[8,64,128]{2,1,0:T(8,128)} %broadcast_in_dim.14), calls=%async_computation.1 | async-start | bytes 524288 | tf_op jit(solution)/shard_map/all_to_all | solution.py:192
  45.5 20.2 %copy-start.1 = (s32[2]{0:T(128)}, s32[2]{0:T(128)S(1)}, u32[]{:S(2)}) copy-start(s32[2]{0:T(128)S(1)} %pad_add_fusion.place_ref) | copy-start | bytes 28
Sparse Core Ops, SparseCore 0:
  9.4 52.3 all-gather.5
  63.9 46.4 all-gather.7

commit v6 on v5

--- a/solution.py
+++ b/solution.py
@@ -44,13 +44,20 @@
     )(panel_one, panel_two)
 
 
-def products_kernel(
-    place_ref, near_ref, mine_ref, seen_ref, keep_ref, send_ref, inner, cross
-):
+def streams(count, parts, shape):
+    def part(j):
+        rest = (0,) * len(shape)
+        return pl.BlockSpec((count // parts, *shape), lambda i: (parts * i + j, *rest))
+
+    return [part(j) for j in range(parts)]
+
+
+def products_kernel(place_ref, *refs):
+    *near_refs, mine_ref, seen_ref, keep_ref, send_ref, inner, cross = refs
     side, core = place_ref[0], place_ref[1]
     step = pl.program_id(0)
-    count = near_ref.shape[0]
-    left = near_ref[...].reshape(count * ROWS, 512)
+    count = mine_ref.shape[0]
+    left = jnp.concatenate([ref[...].reshape(-1, 512) for ref in near_refs])
     right = jnp.concatenate(
         [
             mine_ref[:, side].reshape(count * ROWS, 128),
@@ -103,7 +110,7 @@
         out_shape=[jax.ShapeDtypeStruct((768, 128), jnp.float32)] * 2,
         in_specs=[
             pl.BlockSpec(memory_space=pltpu.SMEM),
-            pl.BlockSpec((count, ROWS, 512), lambda i: (i, 0, 0)),
+            *streams(count, 1, (ROWS, 512)),
             pl.BlockSpec((count, 2, ROWS, 128), lambda i: (i, 0, 0, 0)),
             pl.BlockSpec((count, ROWS, 128), lambda i: (i, 0, 0)),
         ],
@@ -126,10 +133,13 @@
 
 
 def update_kernel(
-    place_ref, near_ref, far_ref, sums_ref, tri_ref, old_ref, out_ref, coeffs
+    place_ref, sums_ref, tri_ref, *refs
 ):
+    *refs, out_ref, coeffs = refs
+    parts = len(refs) // 3
+    near_refs, far_refs, old_refs = refs[:parts], refs[parts : 2 * parts], refs[2 * parts :]
     side = place_ref[0]
-    count = near_ref.shape[0]
+    count = near_refs[0].shape[0]
 
     @pl.when(pl.program_id(0) == 0)
     def _():
@@ -145,10 +155,11 @@
         coeffs[256:] = coeff_two
 
     right = split(coeffs[...])
-    for ref, which in ((near_ref, side), (far_ref, 1 - side)):
-        panel = ref[...].reshape(count * ROWS, 512)
-        change = triple(split(panel), right).reshape(count, ROWS, 128)
-        out_ref[:, which] = old_ref[:, which] - change
+    for j, old_ref in enumerate(old_refs):
+        for ref, which in ((near_refs[j], side), (far_refs[j], 1 - side)):
+            panel = ref[...].reshape(count * ROWS, 512)
+            change = triple(split(panel), right).reshape(count, ROWS, 128)
+            out_ref[pl.ds(j * count, count), which] = old_ref[:, which] - change
 
 
 def update(place, near, far, sums, tri, by_owner):
@@ -159,17 +170,17 @@
         out_shape=jax.ShapeDtypeStruct(by_owner.shape, jnp.float32),
         in_specs=[
             pl.BlockSpec(memory_space=pltpu.SMEM),
-            pl.BlockSpec((count, ROWS, 512), lambda i: (i, 0, 0)),
-            pl.BlockSpec((count, ROWS, 512), lambda i: (i, 0, 0)),
             pl.BlockSpec((2, 512, 128), lambda i: (0, 0, 0)),
             pl.BlockSpec((2, 256, 256), lambda i: (0, 0, 0)),
-            pl.BlockSpec((count, 2, ROWS, 128), lambda i: (i, 0, 0, 0)),
+            *streams(count, 4, (ROWS, 512)),
+            *streams(count, 4, (ROWS, 512)),
+            *streams(count, 4, (2, ROWS, 128)),
         ],
         out_specs=pl.BlockSpec((count, 2, ROWS, 128), lambda i: (i, 0, 0, 0)),
         scratch_shapes=[pltpu.VMEM((512, 128), jnp.float32)],
         compiler_params=pltpu.CompilerParams(vmem_limit_bytes=60 * MIB),
         name="update",
-    )(place, near, far, sums, tri, by_owner)
+    )(place, sums, tri, *[near] * 4, *[far] * 4, *[by_owner] * 4)
 
 
 def shards(vectors, panel_one, factor_one, panel_two, factor_two):

time: 127 us -> 126 us (level)
  transfers between devices with their start and end apart: 5 -> 5, of which waited for: 2 -> 2; matrix products, arithmetic and copies ran while one was open for 2% -> 3% of each run, Pallas kernels for 3% -> 3%
where the time goes in v6:
time: 126 us
  blocking collectives  69 us (55%)
  starting transfers between devices  17.8 us (14%)
  between operations  13.6 us (11%)
  Pallas kernels  12 us (10%)
  waiting for transfers between devices  9.72 us (8%)
  local copies, waits for them, and re-layouts  2.95 us (2%)
    all_to_all x1, blocking collectives, shards(): parts = lax.all_to_all(parts, ('xl', 'z', 'xh'), 0, 0)  25.8 us
    all_to_all x1, blocking collectives, shards(): tri = lax.all_to_all(tri, ('y', 'xh'), 0, 0).reshape(64, 128)  15.9 us
    all_to_all x1, blocking collectives, shards(): part = lax.all_to_all(spread, ('xl', 'z'), 0, 0)  12.7 us
    all_to_all x1, starting transfers between devices, shards(): tri = lax.all_to_all(tri, 'z', 0, 0).reshape(8, 16, 2, 256)  10.1 us
    all_to_all x1, waiting for transfers between devices, shards(): tri = lax.all_to_all(tri, 'z', 0, 0).reshape(8, 16, 2, 256)  9.36 us
    ppermute x2, starting transfers between devices, swap(): return lax.ppermute(value, axis, [(0, 1), (1, 0)])  7.72 us
    all_gather x1, blocking collectives, shards(): tri = lax.all_gather(tri, 'core', axis=0)  6.18 us
    pallas_call x1, Pallas kernels, update(): pl.pallas_call(update_kernel, grid=(NY // count,), out_shape=jax.ShapeDty...  6.08 us
  transfers between devices with their start and end apart: 5, of which 2 were waited for; matrix products, arithmetic and copies ran while one was open for 3% of the time, Pallas kernels for 3%

profile of v6, /device:TPU:1, one launch (start us, length us, event | category | flops | bytes accessed | tf_op | source)
XLA Modules:
  0.0 126.0 jit_solution(16709545399966444552)
XLA Ops:
  6.5 0.0 copy-start
  6.5 0.0 all-gather.6.cloned.1.call-start
  6.5 1.9 %pack.1 = f32[192,512]{1,0:T(8,128)} custom-call(f32[192,256]{1,0:T(8,128)} %one_ref.1, f32[192,256]{1,0:T(8,128)} %two_ref.1), custom_call_target="tpu_custom_call" | custom-call | tf_op jit(solution)/shard_map/pack/pallas_call | solution.py:38
  8.5 0.0 all-gather.6.cloned.1.call-update
  8.5 0.0 all-gather.8.cloned.1.call-start
  8.6 5.5 %collective-permute-start = (f32[192,512]{1,0:T(8,128)}, f32[192,512]{1,0:T(8,128)S(1)}, u32[]{:S(2)}, u32[]{:S(2)}) collective-permute-start(f32[192,512]{1,0:T(8,128)} %pack.1), channel_id=1, source_target_pairs={{0,1},{1,0},{2,3},{3,2},{4,5},{5,4},{6,7},{7,6},{8,9},{9,8},{10,11... | collective-permute-start | bytes 1179656 | tf_op jit(solution)/shard_map/ppermute | solution.py:19
  14.1 0.7 broadcast_select_fusion
  14.8 15.9 %all_to_all.20 = f32[16,4,128]{2,1,0:T(4,128)S(1)} all-to-all(f32[16,4,128]{2,1,0:T(4,128)S(1)} %broadcast_in_dim.13), channel_id=1, replica_groups=mesh['xl'=2,'z'=8,'core'=2,'y'=8,'xh'=2] {'y','xh'}, dimensions={0} | all-to-all | bytes 65536 | tf_op jit(solution)/shard_map/all_to_all | solution.py:199
  30.7 0.0 collective-permute-done
  30.7 0.0 copy-start.2
  30.7 0.7 copy-done.2
  31.4 0.0 all-gather.8.cloned.1.call-update
  31.5 0.0 copy-done
  31.5 0.9 dynamic-slice_bitcast_fusion
  32.4 2.2 %collective-permute-start.1 = (f32[8,192,128]{2,1,0:T(8,128)}, f32[8,192,128]{2,1,0:T(8,128)S(1)}, u32[]{:S(2)}, u32[]{:S(2)}) collective-permute-start(f32[8,192,128]{2,1,0:T(8,128)} %dynamic-slice_bitcast_fusion), channel_id=1, source_target_pairs={{0,1},{1,0},{2,3},{3,2},{4,5},{5,4},{6,7},{7,6},{8,9},{9,8},{10,11... | collective-permute-start | bytes 2359304 | tf_op jit(solution)/shard_map/ppermute | solution.py:19
  34.7 0.7 broadcast_in_dim.14
  35.4 10.1 %all-to-all-start.1 = ((f32[8,64,128]{2,1,0:T(8,128)}), f32[8,64,128]{2,1,0:T(8,128)S(1)}, u32[]{:S(2)}, u32[]{:S(2)}) async-start(f32[8,64,128]{2,1,0:T(8,128)} %broadcast_in_dim.14), calls=%async_computation.1 | async-start | bytes 524288 | tf_op jit(solution)/shard_map/all_to_all | solution.py:203
  45.4 0.1 pad_add_fusion.place_ref
  45.5 0.0 copy-start.1
  45.5 9.4 %all-to-all-done.1 = f32[8,64,128]{2,1,0:T(8,128)S(1)} async-done(((f32[8,64,128]{2,1,0:T(8,128)}), f32[8,64,128]{2,1,0:T(8,128)S(1)}, u32[]{:S(2)}, u32[]{:S(2)}) %all-to-all-start.1) | async-done | bytes 262176 | tf_op jit(solution)/shard_map/all_to_all | solution.py:203
  54.9 0.2 reshape.30
  55.0 0.1 copy.10
  55.1 0.2 all_gather_reshape.6
  55.3 6.2 %all_gather.26.tri_ref = f32[2,256,256]{2,1,0:T(8,128)} all-gather(f32[1,256,256]{2,1,0:T(8,128)S(1)} %all_gather_reshape.6), channel_id=1, replica_groups=mesh['xl'=2,'z'=8,'core'=2,'y'=8,'xh'=2] {'core'}, dimensions={0}, use_global_device_ids=true | all-gather | bytes 786432 | tf_op jit(solution)/shard_map/all_gather | solution.py:205
  61.5 0.3 all-gather.6.cloned.1.call-done
  61.8 0.0 collective-permute-done.1.refs_2_
  61.8 3.9 %products.1 = (f32[768,128]{1,0:T(8,128)S(1)}, f32[768,128]{1,0:T(8,128)S(1)}) custom-call(s32[2]{0:T(128)S(1)} %pad_add_fusion.place_ref, f32[8,192,512]{2,1,0:T(8,128)} %bitcast.31, f32[8,2,192,128]{3,2,1,0:T(8,128)S(1)} %bitcast.30, f32[8,192,128]{2,1,0:T(8,128)S(1)} %collective-permute-done.1.refs_2_), custom_call_target="tpu_custom_call" | custom-call | tf_op jit(solution)/shard_map/products/pallas_call | solution.py:107
  65.7 0.0 copy-done.1
  65.8 3.3 %all-gather.1 = f32[1536,128]{1,0:T(8,128)S(1)} all-gather(f32[768,128]{1,0:T(8,128)S(1)} %get-tuple-element.16), channel_id=3, replica_groups=mesh['xl'=2,'z'=8,'core'=2,'y'=8,'xh'=2] {'core'}, dimensions={0}, use_global_device_ids=true | all-gather | bytes 1179648 | tf_op jit(solution)/shard_map/all_gather | solution.py:209
  69.2 0.1 pad_maximum_fusion
  69.3 25.8 %all_to_all.21 = f32[32,32,128]{2,1,0:T(8,128)S(1)} all-to-all(f32[32,32,128]{2,1,0:T(8,128)S(1)} %bitcast.40), channel_id=1, replica_groups=mesh['xl'=2,'z'=8,'core'=2,'y'=8,'xh'=2] {'xl','z','xh'}, dimensions={0} | all-to-all | bytes 1048576 | tf_op jit(solution)/shard_map/all_to_all | solution.py:214
  95.1 12.7 %all_to_all.22 = f32[16,32,128]{2,1,0:T(8,128)S(1)} all-to-all(f32[16,32,128]{2,1,0:T(8,128)S(1)} %broadcast_in_dim.32), channel_id=1, replica_groups=mesh['xl'=2,'z'=8,'core'=2,'y'=8,'xh'=2] {'xl','z'}, dimensions={0} | all-to-all | bytes 524288 | tf_op jit(solution)/shard_map/all_to_all | solution.py:216
  107.8 5.3 %all_gather.29.sums_ref = f32[2,512,128]{2,1,0:T(8,128)} all-gather(f32[1,512,128]{2,1,0:T(8,128)S(1)} %bitcast.42), channel_id=1, replica_groups=mesh['xl'=2,'z'=8,'core'=2,'y'=8,'xh'=2] {'core'}, dimensions={0}, use_global_device_ids=true | all-gather | bytes 786432 | tf_op jit(solution)/shard_map/all_gather | solution.py:218
  113.1 0.0 all-gather.8.cloned.1.call-done
  113.1 6.1 %update.1 = f32[8,2,192,128]{3,2,1,0:T(8,128)} custom-call(s32[2]{0:T(128)} %copy-done.1, f32[2,512,128]{2,1,0:T(8,128)} %all_gather.29.sums_ref, f32[2,256,256]{2,1,0:T(8,128)} %all_gather.26.tri_ref, f32[8,192,512]{2,1,0:T(8,128)} %bitcast.32, f32[8,192,512]{2,1,0:T(8,128)} %bitcast.33, f32[8,192,512]{2,1,0:T(8,128)} %bitcast.34, f32[8,192,512]{2,1,0:T(8,128)} %bitcast.35, ...), custom_call_target="tpu_custom_call" | custom-call | tf_op jit(solution)/shard_map/update/pallas_call | solution.py:167
  (11 shorter events, 0.2 us)
Async XLA Ops:
  6.5 24.9 %copy-start = (f32[3072,128]{1,0:T(8,128)S(1)}, f32[3072,128]{1,0:T(8,128)}, u32[]{:S(2)}) copy-start(f32[3072,128]{1,0:T(8,128)} %param.5) | copy-start | bytes 4718596
  6.5 55.3 %all-gather.6.cloned.1.call-start = ((), (), s32[]{:S(2)}) async-start(), calls=%async_computation.4 | async-start | bytes 3538944 | tf_op jit(solution)/shard_map/all_gather | solution.py:191
  8.5 104.6 %all-gather.8.cloned.1.call-start = ((), (), s32[]{:S(2)}) async-start(), calls=%async_computation.5 | async-start | bytes 3538944 | tf_op jit(solution)/shard_map/all_gather | solution.py:201
  8.6 22.1 %collective-permute-start = (f32[192,512]{1,0:T(8,128)}, f32[192,512]{1,0:T(8,128)S(1)}, u32[]{:S(2)}, u32[]{:S(2)}) collective-permute-start(f32[192,512]{1,0:T(8,128)} %pack.1), channel_id=1, source_target_pairs={{0,1},{1,0},{2,3},{3,2},{4,5},{5,4},{6,7},{7,6},{8,9},{9,8},{10,11... | collective-permute-start | bytes 1179656 | tf_op jit(solution)/shard_map/ppermute | solution.py:19
  30.7 0.7 copy-start.2
  32.4 29.4 %collective-permute-start.1 = (f32[8,192,128]{2,1,0:T(8,128)}, f32[8,192,128]{2,1,0:T(8,128)S(1)}, u32[]{:S(2)}, u32[]{:S(2)}) collective-permute-start(f32[8,192,128]{2,1,0:T(8,128)} %dynamic-slice_bitcast_fusion), channel_id=1, source_target_pairs={{0,1},{1,0},{2,3},{3,2},{4,5},{5,4},{6,7},{7,6},{8,9},{9,8},{10,11... | collective-permute-start | bytes 2359304 | tf_op jit(solution)/shard_map/ppermute | solution.py:19
  35.4 19.5 %all-to-all-start.1 = ((f32[8,64,128]{2,1,0:T(8,128)}), f32[8,64,128]{2,1,0:T(8,128)S(1)}, u32[]{:S(2)}, u32[]{:S(2)}) async-start(f32[8,64,128]{2,1,0:T(8,128)} %broadcast_in_dim.14), calls=%async_computation.1 | async-start | bytes 524288 | tf_op jit(solution)/shard_map/all_to_all | solution.py:203
  45.5 20.2 %copy-start.1 = (s32[2]{0:T(128)}, s32[2]{0:T(128)S(1)}, u32[]{:S(2)}) copy-start(s32[2]{0:T(128)S(1)} %pad_add_fusion.place_ref) | copy-start | bytes 28
Sparse Core Ops, SparseCore 0:
  9.4 52.3 all-gather.5
  63.9 46.4 all-gather.7

commit v7 on v6

--- a/solution.py
+++ b/solution.py
@@ -96,10 +96,10 @@
     def _():
         for out_ref, which in ((keep_ref, core), (send_ref, 1 - core)):
             own, far = inner[which, :, :128], inner[which, :, 128:]
-            out_ref[:256] = jnp.where(side == 0, own, far)
-            out_ref[256:512] = jnp.where(side == 0, far, own)
-            out_ref[512:640] = cross[which, :, :128]
-            out_ref[640:] = cross[which, :, 128:]
+            out_ref[:, 0] = jnp.where(side == 0, own, far).reshape(16, 16, 128)
+            out_ref[:, 1] = jnp.where(side == 0, far, own).reshape(16, 16, 128)
+            out_ref[:8, 2] = cross[which, :, :128].reshape(8, 16, 128)
+            out_ref[8:, 2] = cross[which, :, 128:].reshape(8, 16, 128)
 
 
 def products(place, near, by_owner, seen):
@@ -107,14 +107,14 @@
     return pl.pallas_call(
         products_kernel,
         grid=(NY // count,),
-        out_shape=[jax.ShapeDtypeStruct((768, 128), jnp.float32)] * 2,
+        out_shape=[jax.ShapeDtypeStruct((16, 3, 16, 128), jnp.float32)] * 2,
         in_specs=[
             pl.BlockSpec(memory_space=pltpu.SMEM),
             *streams(count, 1, (ROWS, 512)),
             pl.BlockSpec((count, 2, ROWS, 128), lambda i: (i, 0, 0, 0)),
             pl.BlockSpec((count, ROWS, 128), lambda i: (i, 0, 0)),
         ],
-        out_specs=[pl.BlockSpec((768, 128), lambda i: (0, 0))] * 2,
+        out_specs=[pl.BlockSpec((16, 3, 16, 128), lambda i: (0, 0, 0, 0))] * 2,
         scratch_shapes=[
             pltpu.VMEM((2, 256, 256), jnp.float32),
             pltpu.VMEM((2, 128, 256), jnp.float32),
@@ -208,9 +208,8 @@
     keep, send = products(place, near, by_owner, seen)
     sent = lax.all_gather(send, "core", axis=0)
     part = keep + lax.dynamic_index_in_dim(sent, 1 - core, 0, False)
-    inner = part[:512].reshape(2, 16, 16, 128).transpose(1, 0, 2, 3)
-    cross = jnp.broadcast_to(part[512:].reshape(16, 1, 16, 128), (16, 2, 16, 128))
-    parts = jnp.concatenate([inner, cross], axis=2).reshape(32, 32, 128)
+    cross = jnp.broadcast_to(part[:, 2:], (16, 2, 16, 128))
+    parts = jnp.concatenate([part[:, :2], cross], axis=2).reshape(32, 32, 128)
     parts = lax.all_to_all(parts, ("xl", "z", "xh"), 0, 0)
     spread = jnp.broadcast_to(parts.sum(0)[None], (16, 32, 128))
     part = lax.all_to_all(spread, ("xl", "z"), 0, 0)

time: 126 us -> 126 us (level)
  transfers between devices with their start and end apart: 5 -> 5, of which waited for: 2 -> 2; matrix products, arithmetic and copies ran while one was open for 3% -> 2% of each run, Pallas kernels for 3% -> 3%
where the time goes in v7:
time: 126 us
  blocking collectives  69 us (55%)
  starting transfers between devices  17.8 us (14%)
  between operations  13.6 us (11%)
  Pallas kernels  12 us (10%)
  waiting for transfers between devices  9.72 us (8%)
  local copies, waits for them, and re-layouts  2.93 us (2%)
    all_to_all x1, blocking collectives, shards(): parts = lax.all_to_all(parts, ('xl', 'z', 'xh'), 0, 0)  25.8 us
    all_to_all x1, blocking collectives, shards(): tri = lax.all_to_all(tri, ('y', 'xh'), 0, 0).reshape(64, 128)  15.9 us
    all_to_all x1, blocking collectives, shards(): part = lax.all_to_all(spread, ('xl', 'z'), 0, 0)  12.7 us
    all_to_all x1, starting transfers between devices, shards(): tri = lax.all_to_all(tri, 'z', 0, 0).reshape(8, 16, 2, 256)  10.1 us
    all_to_all x1, waiting for transfers between devices, shards(): tri = lax.all_to_all(tri, 'z', 0, 0).reshape(8, 16, 2, 256)  9.36 us
    ppermute x2, starting transfers between devices, swap(): return lax.ppermute(value, axis, [(0, 1), (1, 0)])  7.72 us
    all_gather x1, blocking collectives, shards(): tri = lax.all_gather(tri, 'core', axis=0)  6.18 us
    pallas_call x1, Pallas kernels, update(): pl.pallas_call(update_kernel, grid=(NY // count,), out_shape=jax.ShapeDty...  6.09 us
  transfers between devices with their start and end apart: 5, of which 2 were waited for; matrix products, arithmetic and copies ran while one was open for 2% of the time, Pallas kernels for 3%

profile of v7, /device:TPU:1, one launch (start us, length us, event | category | flops | bytes accessed | tf_op | source)
XLA Modules:
  0.0 126.0 jit_solution(17371040800439041833)
XLA Ops:
  6.5 0.0 copy-start
  6.5 0.0 all-gather.6.cloned.1.call-start
  6.5 1.9 %pack.1 = f32[192,512]{1,0:T(8,128)} custom-call(f32[192,256]{1,0:T(8,128)} %one_ref.1, f32[192,256]{1,0:T(8,128)} %two_ref.1), custom_call_target="tpu_custom_call" | custom-call | tf_op jit(solution)/shard_map/pack/pallas_call | solution.py:38
  8.5 0.0 all-gather.6.cloned.1.call-update
  8.5 0.0 all-gather.8.cloned.1.call-start
  8.6 5.5 %collective-permute-start = (f32[192,512]{1,0:T(8,128)}, f32[192,512]{1,0:T(8,128)S(1)}, u32[]{:S(2)}, u32[]{:S(2)}) collective-permute-start(f32[192,512]{1,0:T(8,128)} %pack.1), channel_id=1, source_target_pairs={{0,1},{1,0},{2,3},{3,2},{4,5},{5,4},{6,7},{7,6},{8,9},{9,8},{10,11... | collective-permute-start | bytes 1179656 | tf_op jit(solution)/shard_map/ppermute | solution.py:19
  14.1 0.7 broadcast_select_fusion
  14.8 15.9 %all_to_all.20 = f32[16,4,128]{2,1,0:T(4,128)S(1)} all-to-all(f32[16,4,128]{2,1,0:T(4,128)S(1)} %broadcast_in_dim.13), channel_id=1, replica_groups=mesh['xl'=2,'z'=8,'core'=2,'y'=8,'xh'=2] {'y','xh'}, dimensions={0} | all-to-all | bytes 65536 | tf_op jit(solution)/shard_map/all_to_all | solution.py:199
  30.7 0.0 collective-permute-done
  30.7 0.0 copy-start.2
  30.7 0.7 copy-done.2
  31.4 0.0 all-gather.8.cloned.1.call-update
  31.5 0.0 copy-done
  31.5 0.9 dynamic-slice_bitcast_fusion
  32.4 2.2 %collective-permute-start.1 = (f32[8,192,128]{2,1,0:T(8,128)}, f32[8,192,128]{2,1,0:T(8,128)S(1)}, u32[]{:S(2)}, u32[]{:S(2)}) collective-permute-start(f32[8,192,128]{2,1,0:T(8,128)} %dynamic-slice_bitcast_fusion), channel_id=1, source_target_pairs={{0,1},{1,0},{2,3},{3,2},{4,5},{5,4},{6,7},{7,6},{8,9},{9,8},{10,11... | collective-permute-start | bytes 2359304 | tf_op jit(solution)/shard_map/ppermute | solution.py:19
  34.7 0.7 broadcast_in_dim.14
  35.4 10.1 %all-to-all-start.1 = ((f32[8,64,128]{2,1,0:T(8,128)}), f32[8,64,128]{2,1,0:T(8,128)S(1)}, u32[]{:S(2)}, u32[]{:S(2)}) async-start(f32[8,64,128]{2,1,0:T(8,128)} %broadcast_in_dim.14), calls=%async_computation.1 | async-start | bytes 524288 | tf_op jit(solution)/shard_map/all_to_all | solution.py:203
  45.4 0.1 pad_add_fusion.place_ref
  45.5 0.0 copy-start.1
  45.5 9.4 %all-to-all-done.1 = f32[8,64,128]{2,1,0:T(8,128)S(1)} async-done(((f32[8,64,128]{2,1,0:T(8,128)}), f32[8,64,128]{2,1,0:T(8,128)S(1)}, u32[]{:S(2)}, u32[]{:S(2)}) %all-to-all-start.1) | async-done | bytes 262176 | tf_op jit(solution)/shard_map/all_to_all | solution.py:203
  54.9 0.2 reshape.25
  55.0 0.1 copy.8
  55.1 0.2 all_gather_reshape.6
  55.3 6.2 %all_gather.26.tri_ref = f32[2,256,256]{2,1,0:T(8,128)} all-gather(f32[1,256,256]{2,1,0:T(8,128)S(1)} %all_gather_reshape.6), channel_id=1, replica_groups=mesh['xl'=2,'z'=8,'core'=2,'y'=8,'xh'=2] {'core'}, dimensions={0}, use_global_device_ids=true | all-gather | bytes 786432 | tf_op jit(solution)/shard_map/all_gather | solution.py:205
  61.5 0.3 all-gather.6.cloned.1.call-done
  61.8 0.0 collective-permute-done.1.refs_2_
  61.8 3.9 %products.1 = (f32[16,3,16,128]{3,2,1,0:T(8,128)S(1)}, f32[16,3,16,128]{3,2,1,0:T(8,128)S(1)}) custom-call(s32[2]{0:T(128)S(1)} %pad_add_fusion.place_ref, f32[8,192,512]{2,1,0:T(8,128)} %bitcast.28, f32[8,2,192,128]{3,2,1,0:T(8,128)S(1)} %bitcast.27, f32[8,192,128]{2,1,0:T(8,128)S(1)} %collective-permute-done.1.refs_2_), custom_call_target="tpu_custom_call" | custom-call | tf_op jit(solution)/shard_map/products/pallas_call | solution.py:107
  65.7 0.0 copy-done.1
  65.8 3.3 %all-gather.1 = f32[32,3,16,128]{3,2,1,0:T(8,128)S(1)} all-gather(f32[16,3,16,128]{3,2,1,0:T(8,128)S(1)} %get-tuple-element.16), channel_id=3, replica_groups=mesh['xl'=2,'z'=8,'core'=2,'y'=8,'xh'=2] {'core'}, dimensions={0}, use_global_device_ids=true | all-gather | bytes 1179648 | tf_op jit(solution)/shard_map/all_gather | solution.py:209
  69.1 0.1 bitcast_add_fusion
  69.2 0.1 pad_maximum_fusion
  69.3 25.8 %all_to_all.21 = f32[32,32,128]{2,1,0:T(8,128)S(1)} all-to-all(f32[32,32,128]{2,1,0:T(8,128)S(1)} %bitcast.37), channel_id=1, replica_groups=mesh['xl'=2,'z'=8,'core'=2,'y'=8,'xh'=2] {'xl','z','xh'}, dimensions={0} | all-to-all | bytes 1048576 | tf_op jit(solution)/shard_map/all_to_all | solution.py:213
  95.1 12.7 %all_to_all.22 = f32[16,32,128]{2,1,0:T(8,128)S(1)} all-to-all(f32[16,32,128]{2,1,0:T(8,128)S(1)} %broadcast_in_dim.32), channel_id=1, replica_groups=mesh['xl'=2,'z'=8,'core'=2,'y'=8,'xh'=2] {'xl','z'}, dimensions={0} | all-to-all | bytes 524288 | tf_op jit(solution)/shard_map/all_to_all | solution.py:215
  107.8 5.3 %all_gather.29.sums_ref = f32[2,512,128]{2,1,0:T(8,128)} all-gather(f32[1,512,128]{2,1,0:T(8,128)S(1)} %bitcast.39), channel_id=1, replica_groups=mesh['xl'=2,'z'=8,'core'=2,'y'=8,'xh'=2] {'core'}, dimensions={0}, use_global_device_ids=true | all-gather | bytes 786432 | tf_op jit(solution)/shard_map/all_gather | solution.py:217
  113.1 0.0 all-gather.8.cloned.1.call-done
  113.1 6.1 %update.1 = f32[8,2,192,128]{3,2,1,0:T(8,128)} custom-call(s32[2]{0:T(128)} %copy-done.1, f32[2,512,128]{2,1,0:T(8,128)} %all_gather.29.sums_ref, f32[2,256,256]{2,1,0:T(8,128)} %all_gather.26.tri_ref, f32[8,192,512]{2,1,0:T(8,128)} %bitcast.29, f32[8,192,512]{2,1,0:T(8,128)} %bitcast.30, f32[8,192,512]{2,1,0:T(8,128)} %bitcast.31, f32[8,192,512]{2,1,0:T(8,128)} %bitcast.32, ...), custom_call_target="tpu_custom_call" | custom-call | tf_op jit(solution)/shard_map/update/pallas_call | solution.py:167
  (9 shorter events, 0.2 us)
Async XLA Ops:
  6.5 24.9 %copy-start = (f32[3072,128]{1,0:T(8,128)S(1)}, f32[3072,128]{1,0:T(8,128)}, u32[]{:S(2)}) copy-start(f32[3072,128]{1,0:T(8,128)} %param.5) | copy-start | bytes 4718596
  6.5 55.3 %all-gather.6.cloned.1.call-start = ((), (), s32[]{:S(2)}) async-start(), calls=%async_computation.4 | async-start | bytes 3538944 | tf_op jit(solution)/shard_map/all_gather | solution.py:191
  8.5 104.6 %all-gather.8.cloned.1.call-start = ((), (), s32[]{:S(2)}) async-start(), calls=%async_computation.5 | async-start | bytes 3538944 | tf_op jit(solution)/shard_map/all_gather | solution.py:201
  8.6 22.1 %collective-permute-start = (f32[192,512]{1,0:T(8,128)}, f32[192,512]{1,0:T(8,128)S(1)}, u32[]{:S(2)}, u32[]{:S(2)}) collective-permute-start(f32[192,512]{1,0:T(8,128)} %pack.1), channel_id=1, source_target_pairs={{0,1},{1,0},{2,3},{3,2},{4,5},{5,4},{6,7},{7,6},{8,9},{9,8},{10,11... | collective-permute-start | bytes 1179656 | tf_op jit(solution)/shard_map/ppermute | solution.py:19
  30.7 0.7 copy-start.2
  32.4 29.4 %collective-permute-start.1 = (f32[8,192,128]{2,1,0:T(8,128)}, f32[8,192,128]{2,1,0:T(8,128)S(1)}, u32[]{:S(2)}, u32[]{:S(2)}) collective-permute-start(f32[8,192,128]{2,1,0:T(8,128)} %dynamic-slice_bitcast_fusion), channel_id=1, source_target_pairs={{0,1},{1,0},{2,3},{3,2},{4,5},{5,4},{6,7},{7,6},{8,9},{9,8},{10,11... | collective-permute-start | bytes 2359304 | tf_op jit(solution)/shard_map/ppermute | solution.py:19
  35.4 19.5 %all-to-all-start.1 = ((f32[8,64,128]{2,1,0:T(8,128)}), f32[8,64,128]{2,1,0:T(8,128)S(1)}, u32[]{:S(2)}, u32[]{:S(2)}) async-start(f32[8,64,128]{2,1,0:T(8,128)} %broadcast_in_dim.14), calls=%async_computation.1 | async-start | bytes 524288 | tf_op jit(solution)/shard_map/all_to_all | solution.py:203
  45.5 20.2 %copy-start.1 = (s32[2]{0:T(128)}, s32[2]{0:T(128)S(1)}, u32[]{:S(2)}) copy-start(s32[2]{0:T(128)S(1)} %pad_add_fusion.place_ref) | copy-start | bytes 28
Sparse Core Ops, SparseCore 0:
  9.4 52.3 all-gather.5
  63.9 46.4 all-gather.7
